TPU v7x, 32 devices: a whole 2x2x4 slice. The times are simulated.
32 devices in a mesh: rows: 8 (over z, y), seq: 4 (over x, core).
Axes of the slice: x: 2, y: 2, z: 4, core: 2. Of those that a mesh axis runs over, the one named last changes fastest.
Arguments:
- tokens: bfloat16 [16, 1024, 1024], P('rows', 'seq'), may hold values from -6 to 6
- bounds: int32 [16, 4], P('rows'), may hold values from 0 to 1023, as said below
- norm1_gain: float32 [1024], replicated, may hold values from 0.25 to 1.75
- norm1_bias: float32 [1024], replicated, may hold values from -1.5 to 1.5
- w_qkv: bfloat16 [1024, 3072], replicated, may hold values from -0.1875 to 0.1875
- w_proj: bfloat16 [1024, 1024], replicated, may hold values from -1.5 to 1.5
- norm2_gain: float32 [1024], replicated, may hold values from 0.25 to 1.75
- norm2_bias: float32 [1024], replicated, may hold values from -1.5 to 1.5
- w_up: bfloat16 [1024, 4096], replicated, may hold values from -0.1875 to 0.1875
- up_bias: float32 [4096], replicated, may hold values from -1.5 to 1.5
- w_down: bfloat16 [4096, 1024], replicated, may hold values from -0.09375 to 0.09375
- down_bias: float32 [1024], replicated, may hold values from -1.5 to 1.5
- cotangent: bfloat16 [16, 1024, 1024], P('rows', 'seq'), may hold values from -6 to 6
Outputs:
- layer_out: bfloat16 [16, 1024, 1024], P('rows', 'seq')
- grad_tokens: float32 [16, 1024, 1024], P('rows', 'seq')
- grad_norm1_gain: float32 [1024], P(('rows', 'seq'))
- grad_norm1_bias: float32 [1024], P(('rows', 'seq'))
- grad_qkv: float32 [1024, 3072], P(('rows', 'seq'))
- grad_proj: float32 [1024, 1024], P(('rows', 'seq'))
- grad_norm2_gain: float32 [1024], P(('rows', 'seq'))
- grad_norm2_bias: float32 [1024], P(('rows', 'seq'))
- grad_up: float32 [1024, 4096], P(('rows', 'seq'))
- grad_up_bias: float32 [4096], P(('rows', 'seq'))
- grad_down: float32 [4096, 1024], P(('rows', 'seq'))
- grad_down_bias: float32 [1024], P(('rows', 'seq'))
Inputs may be any that keep to these rules, and one draw needn't show every extreme that they name: `bounds`: each row lists the first positions of its 4 documents in increasing order, the first being 0. In every aligned block of 2 rows one row has a document that begins within its first 256 positions and ends within its last 256.
All inputs are finite; a program needn't handle non-finite values.
Results may differ from a plain program's by a relative error of at most 0.007.
Values may be sent and summed in bfloat16 or wider, within the bound.
No kernel may reach another device: no remote copies, remote signals or barrier semaphores. Data moves between devices by JAX's collectives and lax.ppermute only.
A program may use at most 256 MiB of HBM per device.

v0:
```python
import functools

import jax
import jax.numpy as jnp
from jax import lax
from jax.experimental import pallas as pl
from jax.experimental.pallas import tpu as pltpu
from jax.sharding import PartitionSpec as P

HEADS = 16
EPS = 1e-05
BF, F32 = jnp.bfloat16, jnp.float32
AXES = ("rows", "seq")
DOWN = (1, 3)
STEPS = (
    "turn", "d1o", "d2o", "d1m", "dn2", "d2m", "n2t", "uo", "d1f", "mixer", "d1f", "merge", "um", "layer", "d2f",
    "d1f", "back", "att", "q1o", "d1f", "d2f", "d1a", "uf", "q1m", "po", "d2f", "q2o", "pm", "dn1", "q2m", "d2f",
    "q1f", "de", "small", "uf", "pf", "small", "q2f", "small", "uf", "pf", "small", "q1f", "small", "q2f", "small",
    "pf", "q1f", "q2f", "uf", "ue", "pf", "pe", "q2f", "q1f", "qe",
)
SUMS = 64
DEPTH = 80
TILE = 512
BEAT = 3


def dot(a, b):
    return jnp.dot(a, b, preferred_element_type=F32)


def dot_nt(a, b):
    return lax.dot_general(a, b, (((1,), (1,)), ((), ())), preferred_element_type=F32)


def dot_tn(a, b):
    return lax.dot_general(a, b, (((0,), (0,)), ((), ())), preferred_element_type=F32)


def iota(shape, dim):
    return lax.broadcasted_iota(jnp.int32, shape, dim)


SMEM = pl.BlockSpec(memory_space=pltpu.SMEM)
WHOLE = pl.BlockSpec(memory_space=pltpu.VMEM)
HBM = pl.BlockSpec(memory_space=pltpu.HBM)


def cut(at, size):
    return pl.ds(pl.multiple_of(at, size), size)


def in_vmem(x):
    return pltpu.with_memory_space_constraint(x, pltpu.VMEM)


def kernel_call(body, scalars, args, outs, scratch=(), far=(), hold=(), fetch=(), time=0.5, limit=4):
    n_in, n_hold, n_fetch, n_out = len(scalars) + len(args) + len(far), len(hold), len(fetch), len(outs)
    every = [(*o, True)[:3] for o in outs]
    every += [(f.shape, f.dtype, True) for f in fetch] + [((8, 128), F32, True)]

    def wrapped(*refs):
        ins, rest = refs[:n_in], refs[n_in + n_hold :]
        sources, rest = rest[:n_fetch], rest[n_fetch:]
        results, targets = rest[:n_out], rest[n_out : n_out + n_fetch]
        token, rest = rest[n_out + n_fetch], rest[n_out + n_fetch + 1 :]
        copies = []
        if n_fetch:
            sems, rest = rest[-1], rest[:-1]
            copies = [pltpu.make_async_copy(a, b, sems.at[k]) for k, (a, b) in enumerate(zip(sources, targets))]
        for copy in copies:
            copy.start()
        token[...] = jnp.zeros_like(token)
        body(*ins, *results, *rest)
        for copy in copies:
            copy.wait()

    shapes = [pltpu.VMEM(s, d) if v else jax.ShapeDtypeStruct(s, d) for s, d, v in every]
    in_hbm = lambda x: pltpu.with_memory_space_constraint(x, pltpu.HBM)
    out = pl.pallas_call(
        wrapped,
        name=body.__qualname__.split(".")[0],
        in_specs=[SMEM] * len(scalars)
        + [WHOLE] * len(args)
        + [HBM] * len(far)
        + [WHOLE] * n_hold
        + [HBM] * n_fetch,
        out_specs=[WHOLE] * len(every),
        out_shape=shapes,
        scratch_shapes=[*scratch, *([pltpu.SemaphoreType.DMA((n_fetch,))] if n_fetch else [])],
        compiler_params=pltpu.CompilerParams(vmem_limit_bytes=limit << 20),
        cost_estimate=pl.CostEstimate(flops=int(time * 1e10), bytes_accessed=1, transcendentals=0),
    )(*scalars, *map(in_vmem, args), *map(in_hbm, far), *map(in_vmem, hold), *map(in_hbm, fetch))
    return out


def normal(x):
    center = x - jnp.mean(x, -1, keepdims=True)
    root = lax.rsqrt(jnp.mean(center * center, -1, keepdims=True) + EPS)
    return center * root, root


def feature(u):
    return jnp.where(u > 0, u + 1.0, jnp.exp(jnp.minimum(u, 0.0)))


def keep_from(lb, row, span):
    last = 0 - span
    for k in range(lb.shape[1]):
        last = jnp.where(lb[row, k] < span, jnp.maximum(last, lb[row, k]), last)
    return last


def carry_to(lb, row, span):
    end = span
    for k in range(lb.shape[1]):
        end = jnp.where(lb[row, k] >= 0, jnp.minimum(end, lb[row, k]), end)
    return end


def block_mask(lb, row, span):
    t, s = iota((span, span), 0), iota((span, span), 1)
    ok = s <= t
    for k in range(lb.shape[1]):
        ok = ok & ((lb[row, k] > t) | (s >= lb[row, k]))
    return ok.astype(F32)


def pack_state(m):
    half = m.shape[0] // 2
    return jnp.where(iota((half, m.shape[1]), 1) < half, m[:half], m[half:])


def unpack_state(c):
    half = c.shape[0]
    left = iota(c.shape, 1) < half
    return jnp.concatenate([jnp.where(left, c, 0.0), jnp.where(left, 0.0, c)], 0)


def split(x):
    hi = x.astype(BF)
    return hi, (x - hi.astype(F32)).astype(BF)


def head_ones(lanes=128):
    half = lanes // 2
    return ((iota((lanes, lanes), 0) < half) == (iota((lanes, lanes), 1) < half)).astype(BF)


def head_sum(x):
    hi, lo = split(x)
    ones = head_ones(x.shape[1])
    return dot(jnp.concatenate([hi, lo], 1), jnp.concatenate([ones, ones], 0))


def dot_split(a, m):
    hi, lo = split(m)
    return dot(jnp.concatenate([a, a], 1), jnp.concatenate([hi, lo], 0))


def keys_values(lb, tokens, vectors, w_qkv, span, **kw):
    count, model = tokens.shape
    rows, width = count // span, 256
    n_vec, blocks = len(vectors), model // 512

    def body(lb, *refs):
        x_in, vec_in, w_in = refs[0], refs[1 : 1 + n_vec], refs[1 + n_vec]
        n1, km, v, own, *vecs = refs[2 + n_vec : 6 + 2 * n_vec]
        x, w, sems = refs[6 + 2 * n_vec :]

        def copy(k, a, b):
            return pltpu.make_async_copy(a, b, sems.at[k])

        def columns(j):
            lanes = slice(j * 512, (j + 1) * 512)
            return copy(1 + n_vec + j, w_in.at[:, model + j * 512 : model + (j + 1) * 512], w.at[:, lanes])

        head = [copy(0, x_in, x)] + [copy(1 + k, a, b) for k, (a, b) in enumerate(zip(vec_in, vecs))]
        for c in head:
            c.start()
        for c in [c for j in range(blocks) for c in (j, blocks + j)]:
            columns(c).start()
        for c in head:
            c.wait()

        @pl.loop(0, count // 64, unroll=2)
        def _(i):
            at = cut(i * 64, 64)
            n1[at] = (normal(x[at].astype(F32))[0] * vecs[0][...] + vecs[1][...]).astype(BF)

        kept = [iota((span, width), 0) >= keep_from(lb, r, span) for r in range(rows)]
        for j in range(model // width):
            if j * width % 512 == 0:
                columns(j * width // 512).wait()
                columns(blocks + j * width // 512).wait()
            lanes = slice(j * width, (j + 1) * width)
            key = feature(dot(n1[...], w[:, lanes])).astype(BF)
            val = dot(n1[...], w[:, model + j * width : model + (j + 1) * width]).astype(BF)
            km[:, lanes], v[:, lanes] = key, val
            for r in range(rows):
                part = slice(r * span, (r + 1) * span)
                owned = jnp.where(kept[r], key[part], jnp.zeros((), BF))
                for p in range(width // 128):
                    at = slice(p * 128, (p + 1) * 128)
                    block = j * (width // 128) + p
                    own[r, block, 0:SUMS] = pack_state(dot_tn(owned[:, at], val[part, at])).astype(BF)
                    total = jnp.sum(owned[:, at].astype(F32), 0, keepdims=True)
                    own[r, block, SUMS:DEPTH] = jnp.broadcast_to(total, (DEPTH - SUMS, 128)).astype(BF)

    wide = ((count, model), BF)
    outs = [wide, wide, wide, ((rows, model // 128, DEPTH, 128), BF)]
    outs += [(v.shape, v.dtype) for v in vectors]
    return kernel_call(
        body, (lb,), (), outs, far=(tokens, *vectors, w_qkv),
        scratch=[
            pltpu.VMEM((count, model), BF),
            pltpu.VMEM((model, 2 * model), BF),
            pltpu.SemaphoreType.DMA((1 + n_vec + 2 * blocks,)),
        ],
        limit=7, time=7.3, **kw,
    )


def merge_states(coefs, own, got, **kw):
    rows = own.shape[0]

    def body(c, a, b, out):
        for r in range(rows):
            out[r] = (c[0, r] * a[r].astype(F32) + c[1, r] * b[r].astype(F32)).astype(BF)

    return kernel_call(body, (coefs,), (own, got), [(own.shape, BF)], **kw)


def queries(normed, w_qkv, tables, shards, **kw):
    count, model = normed.shape
    tiles = model // TILE

    def body(tables, n, w_in, q, n_t, w, sems):
        copies = [
            pltpu.make_async_copy(w_in.at[:, j * TILE : (j + 1) * TILE], w.at[:, j * TILE : (j + 1) * TILE], sems.at[j])
            for j in range(tiles)
        ]
        for c in copies:
            c.start()
        turn(tables, n, n_t, model // shards)
        for j in range(tiles):
            lanes = slice(j * TILE, (j + 1) * TILE)
            copies[j].wait()
            q[:, lanes] = feature(dot(n[...], w[:, lanes])).astype(BF)

    return kernel_call(
        body, (tables,), (normed,), [((count, model), BF), ((model, count), BF)], far=(w_qkv,),
        scratch=[pltpu.VMEM((model, model), BF), pltpu.SemaphoreType.DMA((tiles,))],
        limit=5, time=3.9, **kw,
    )


def active_grads(cotangent, w_down, **kw):
    count, model = cotangent.shape
    ff = w_down.shape[0]

    def body(c, w, out):
        for j in range(ff // TILE):
            lanes = slice(j * TILE, (j + 1) * TILE)
            out[:, lanes] = dot_nt(c[...], w[lanes, :]).astype(BF)

    return kernel_call(
        body, (), (cotangent, w_down), [((count, ff), BF)], time=4.5, **kw
    )


def attend_inside(lb, query, key, values, span, **kw):
    count, model = query.shape
    rows = count // span

    def body(lb, q_ref, k_ref, v_ref, numer, denom, mask):
        for r in range(rows):
            mask[r] = block_mask(lb, r, span)
        left = iota((span, 128), 1) < 64
        zero = jnp.zeros((), BF)

        @pl.loop(0, model // 128, unroll=4)
        def _(p):
            lanes = cut(p * 128, 128)
            for r in range(rows):
                part = slice(r * span, (r + 1) * span)
                q, k, v = q_ref[part, lanes], k_ref[part, lanes], v_ref[part, lanes]
                total = 0.0
                for e in range(2):
                    mine = left if e == 0 else ~left
                    scores = dot_nt(jnp.where(mine, q, zero), k)
                    weights = (scores * mask[r]).astype(BF)
                    both = jnp.concatenate([jnp.where(mine, v, zero), mine.astype(BF)], 1)
                    total = total + dot(weights, both)
                numer[part, lanes] = total[:, :128]
                denom[part, lanes] = total[:, 128:]

    wide = ((count, model), F32)
    return kernel_call(
        body, (lb,), (query, key, values), [wide, wide],
        scratch=[pltpu.VMEM((rows, span, span), F32)], time=5.7, **kw,
    )


def state_of(coefs, gots, r, p):
    total = 0.0
    for i, got in enumerate(gots):
        total = total + coefs[i, r] * got[r, p].astype(F32)
    return total


def attend_join(lb, coefs, gots, query, numer, denom, tokens, w_proj, gain, bias, span, **kw):
    count, model = query.shape
    pairs, n = model // 128, len(gots)
    rows = count // span

    def body(lb, coefs, *refs):
        gots, (q_ref, num_ref, den_ref, x, w, g, b, att, rden, middle, n2) = refs[:n], refs[n:]
        place = iota((span, 128), 0)

        @pl.loop(0, pairs, unroll=4)
        def _(p):
            lanes = cut(p * 128, 128)
            for r in range(rows):
                part = slice(r * span, (r + 1) * span)
                state = state_of(coefs, gots, r, p)
                q = jnp.where(place < carry_to(lb, r, span), q_ref[part, lanes], jnp.zeros((), BF))
                num = num_ref[part, lanes] + dot_split(q, unpack_state(state[0:SUMS]))
                den = den_ref[part, lanes] + head_sum(q.astype(F32) * state[SUMS : SUMS + 1])
                inv = 1.0 / den
                rden[part, lanes] = inv
                att[part, lanes] = (num * inv).astype(BF)

        for j in range(model // 256):
            lanes = slice(j * 256, (j + 1) * 256)
            middle[:, lanes] = x[:, lanes].astype(F32) + dot(att[...], w[:, lanes])

        @pl.loop(0, count // 64, unroll=2)
        def _(i):
            at = cut(i * 64, 64)
            n2[at] = (normal(middle[at])[0] * g[...] + b[...]).astype(BF)

    wide = (count, model)
    return kernel_call(
        body, (lb, coefs), (*gots, query, numer, denom, tokens, w_proj, gain, bias),
        [(wide, BF), (wide, F32), (wide, F32), (wide, BF)],
        time=5.0, **kw,
    )


def expand(normed, w_up, up_bias, d_active, **kw):
    count, model = normed.shape
    ff = w_up.shape[1]
    c0, c1 = 0.7978845608028654, 0.7978845608028654 * 0.044715
    step = 32

    def body(n, w, b, da, hid, dp, total, even, odd):
        ones = jnp.ones((16, count), BF)

        def product(j, out):
            out[...] = dot(n[...], w[:, cut(j * TILE, TILE)])

        def rest(j, u_ref):
            lanes = cut(j * TILE, TILE)
            bias = b[:, lanes]
            for i in range(count // step):
                at = slice(i * step, (i + 1) * step)
                u = u_ref[at] + bias
                z = u * (c0 + c1 * (u * u))
                t = jnp.tanh(z)
                rise = 0.5 + 0.5 * t
                hid[at, lanes] = (u * rise).astype(BF)
                slope = rise * (1.0 + (1.0 - t) * (3.0 * z - (2.0 * c0) * u))
                dp[at, lanes] = (slope * da[at, lanes].astype(F32)).astype(BF)
            total[:, lanes] = dot(ones, dp[:, lanes])[0:1]

        tiles = ff // TILE
        product(0, even)

        @pl.loop(0, tiles // 2 - 1)
        def _(i):
            product(2 * i + 1, odd)
            rest(2 * i, even)
            product(2 * i + 2, even)
            rest(2 * i + 1, odd)

        product(tiles - 1, odd)
        rest(tiles - 2, even)
        rest(tiles - 1, odd)

    wide = ((count, ff), BF)
    return kernel_call(
        body, (), (normed, w_up, up_bias, d_active), [wide, wide, ((1, ff), F32)],
        scratch=[pltpu.VMEM((count, TILE), F32)] * 2, limit=6, time=11.0, **kw,
    )


def turn(tables, x, out, deep):
    for j in range(x.shape[1] // 128):
        t = x[:, j * 128 : (j + 1) * 128].T
        for k in range(128 // deep):
            out[cut(tables[2, j * (128 // deep) + k] * deep, deep), :] = t[k * deep : (k + 1) * deep]


def turned(x, tables, shards, **kw):
    count, model = x.shape
    deep = model // shards

    def body(tables, x, out):
        turn(tables, x, out, deep)

    return kernel_call(body, (tables,), (x,), [((model, count), BF)], **kw)


def weight_grad(lhs_t, rhs, first, steps, side, tables, got=None, **kw):
    deep, count = lhs_t.shape
    shards = tables.shape[1]
    rows, half = deep // shards, deep // 2
    time = 0.9 * steps
    shape = (deep, TILE * steps)

    def tile(b, which, j):
        return b[:, cut((which * side + first + j) * TILE, TILE)]

    if got is None:

        def body(tables, a, b, out):
            for j in range(steps):
                total = dot(a[...], tile(b, 1 - tables[3, 0], j)).astype(BF)
                for k in range(shards):
                    at = (k & 0b01010) | (k >> 4 & 1) << 2 | (k >> 2 & 1) << 4 | (~k & 1)
                    out[at * rows : (at + 1) * rows, j * TILE : (j + 1) * TILE] = total[k * rows : (k + 1) * rows]

        return kernel_call(body, (tables,), (lhs_t, rhs), [(shape, BF)], time=time, **kw)

    def body(tables, a, b, g, send, keep):
        for j in range(steps):
            lanes = slice(j * TILE, (j + 1) * TILE)
            total = dot(a[...], tile(b, tables[3, 0], j)) + g[:, lanes].astype(F32)
            send[:, lanes] = total[:half].astype(BF)
            keep[:, lanes] = total[half:].astype(BF)

    return kernel_call(
        body, (tables,), (lhs_t, rhs, got), [((half, TILE * steps), BF)] * 2, limit=9, time=time, **kw
    )


def transposed(x, **kw):
    def body(x, out):
        for j in range(x.shape[1] // TILE):
            out[j * TILE : (j + 1) * TILE, :] = x[:, j * TILE : (j + 1) * TILE].T

    return kernel_call(body, (), (x,), [(x.shape[::-1], x.dtype)], time=2.0, **kw)


def down_grad(hidden_t, cotangent, width, first, side, tables, got=None, **kw):
    ff, count = hidden_t.shape
    shards = tables.shape[1]
    deep = ff // shards
    per = TILE // deep
    steps = ff // TILE
    time = width / 110

    def product(tables, h, c, i, mine):
        which = 0 if mine else 1
        core = tables[3, 0]
        column = pl.multiple_of((core if mine else 1 - core) * side + first, 128)
        lhs = [h[cut(tables[which, per * i + k] * deep, deep), :] for k in range(per)]
        return dot(jnp.concatenate(lhs, 0), c[:, pl.ds(column, width)])

    if got is None:

        def body(tables, h, c, out):
            for i in range(steps):
                out[i * TILE : (i + 1) * TILE] = product(tables, h, c, i, False).astype(BF)

        return kernel_call(body, (tables,), (hidden_t, cotangent), [((ff, width), BF)], time=time, **kw)

    def body(tables, h, c, g, send, keep):
        for i in range(steps):
            total = product(tables, h, c, i, True) + g[i * TILE : (i + 1) * TILE].astype(F32)
            out, at = (send, i) if i < steps // 2 else (keep, i - steps // 2)
            out[at * TILE : (at + 1) * TILE] = total.astype(BF)

    return kernel_call(
        body, (tables,), (hidden_t, cotangent, got), [((ff // 2, width), BF)] * 2, limit=6, time=time, **kw
    )


def norm_grad_rows(e_ref, x_of, gain, count, write):
    step, model = 32, gain.shape[1]

    def one(i, sums):
        at = cut(i * step, step)
        e = e_ref[at]
        hat, root = normal(x_of(at))
        g = e * gain[...]
        back = root * (g - jnp.mean(g, -1, keepdims=True) - hat * jnp.mean(g * hat, -1, keepdims=True))
        write(at, back)
        eights = lambda v: jnp.sum(v.reshape(step // 8, 8, model), 0)
        return sums[0] + eights(e * hat), sums[1] + eights(e)

    zero = jnp.zeros((8, model), F32)
    sums = lax.fori_loop(0, count // step, one, (zero, zero), unroll=4)
    return [jnp.sum(s, 0, keepdims=True) for s in sums]


def second_norm_grads(d_pre, w_up, middle, cotangent, gain, **kw):
    count, ff = d_pre.shape
    model = w_up.shape[0]

    def body(d, w, mid, cot, g, d_mid, branch, g_gain, g_bias, g_down, e):
        for j in range(model // 256):
            lanes = slice(j * 256, (j + 1) * 256)
            e[:, lanes] = dot_nt(d[...], w[lanes, :])

        def write(at, back):
            out = cot[at].astype(F32) + back
            d_mid[at] = out
            branch[at] = out.astype(BF)

        g_gain[...], g_bias[...] = norm_grad_rows(e, lambda at: mid[at], g, count, write)
        g_down[...] = jnp.sum(cot[...].astype(F32), 0, keepdims=True)

    vec, wide = ((1, model), F32), (count, model)
    return kernel_call(
        body, (), (d_pre, w_up, middle, cotangent, gain), [(wide, F32), (wide, BF), vec, vec, vec],
        scratch=[pltpu.VMEM(wide, F32)], time=7.0, **kw,
    )


def mixer_grads(lb, branch, w_proj, attended, rden, query, span, **kw):
    count, model = branch.shape
    rows, pairs = count // span, model // 128

    def body(lb, br, w, att, rd, q_ref, dn, dd, own):
        place = iota((span, 128), 0)
        for j in range(model // 256):
            d_att = dot_nt(br[...], w[j * 256 : (j + 1) * 256, :])
            for k in range(2):
                p = 2 * j + k
                lanes = slice(p * 128, (p + 1) * 128)
                for r in range(rows):
                    part = slice(r * span, (r + 1) * span)
                    d, inv = d_att[part, k * 128 : (k + 1) * 128], rd[part, lanes]
                    d_den = -head_sum(d * att[part, lanes].astype(F32)) * inv
                    d_num = (d * inv).astype(BF)
                    dn[part, lanes], dd[part, lanes] = d_num, d_den
                    q = jnp.where(place < carry_to(lb, r, span), q_ref[part, lanes], jnp.zeros((), BF))
                    own[r, p, 0:SUMS] = pack_state(dot_tn(q, d_num)).astype(BF)
                    total = jnp.sum(d_den * q.astype(F32), 0, keepdims=True)
                    own[r, p, SUMS:DEPTH] = jnp.broadcast_to(total, (DEPTH - SUMS, 128)).astype(BF)

    wide = (count, model)
    return kernel_call(
        body, (lb,), (branch, w_proj, attended, rden, query),
        [(wide, BF), (wide, F32), ((rows, pairs, DEPTH, 128), BF)],
        time=5.0, **kw,
    )


def attend_back(lb, coefs, back_coefs, gots, back_gots, query, key, values, d_num, d_den, span, **kw):
    count, model = query.shape
    rows, n, m = count // span, len(gots), len(back_gots)

    def body(lb, coefs, back_coefs, *refs):
        gots, back_gots = refs[:n], refs[n : n + m]
        q_ref, k_ref, v_ref, dn_ref, dd_ref, out, mask, mask_t = refs[n + m :]
        for r in range(rows):
            ok = block_mask(lb, r, span)
            mask[r], mask_t[r] = ok, ok.T
        lane, place = iota((span, 128), 1), iota((span, 128), 0)
        left = lane < 64
        zero = jnp.zeros((), BF)

        @pl.loop(0, model // 128, unroll=4)
        def _(p):
            lanes = cut(p * 128, 128)
            for r in range(rows):
                part = slice(r * span, (r + 1) * span)
                carried = place < carry_to(lb, r, span)
                kept = place >= keep_from(lb, r, span)
                q, k, v = q_ref[part, lanes], k_ref[part, lanes], v_ref[part, lanes]
                dn, dd = dn_ref[part, lanes], dd_ref[part, lanes]
                hi, lo = split(dd)
                v_ones = jnp.concatenate([v, jnp.ones_like(v)], 1)
                dq = dk = dv = 0.0
                for e in range(2):
                    mine = left if e == 0 else ~left
                    at = 64 * e
                    qm, dnm = jnp.where(mine, q, zero), jnp.where(mine, dn, zero)
                    extra = jnp.where(lane == at, hi, jnp.where(lane == at + 1, lo, zero))
                    dn_den = jnp.concatenate([dnm, extra], 1)
                    ds = (dot_nt(dn_den, v_ones) * mask[r]).astype(BF)
                    w_t = (dot_nt(k, qm) * mask_t[r]).astype(BF)
                    dq = dq + dot(ds, jnp.where(mine, k, zero))
                    dk = dk + dot_tn(ds, qm)
                    dv = dv + dot(w_t, dnm)
                state, own = state_of(coefs, gots, r, p), state_of(back_coefs, back_gots, r, p)
                s_hi, s_lo = split(unpack_state(state[0:SUMS]))
                o_hi, o_lo = split(unpack_state(own[0:SUMS]))
                through_s = dot_nt(jnp.concatenate([dn, dn], 1), jnp.concatenate([s_hi, s_lo], 1))
                through_o = dot_nt(jnp.concatenate([v, v], 1), jnp.concatenate([o_hi, o_lo], 1))
                through_k = dot(jnp.concatenate([k, k], 1), jnp.concatenate([o_hi, o_lo], 0))
                dq = dq + jnp.where(carried, through_s + dd * state[SUMS : SUMS + 1], 0.0)
                dk = dk + jnp.where(kept, through_o + own[SUMS : SUMS + 1], 0.0)
                dv = dv + jnp.where(kept, through_k, 0.0)
                out[part, lanes] = (dq * jnp.minimum(q.astype(F32), 1.0)).astype(BF)
                out[part, cut(model + p * 128, 128)] = (dk * jnp.minimum(k.astype(F32), 1.0)).astype(BF)
                out[part, cut(2 * model + p * 128, 128)] = dv.astype(BF)

    return kernel_call(
        body, (lb, coefs, back_coefs), (*gots, *back_gots, query, key, values, d_num, d_den),
        [((count, 3 * model), BF)],
        scratch=[pltpu.VMEM((rows, span, span), F32)] * 2, time=12.0, **kw,
    )


def first_norm_grads(d_mixed, w_qkv, tokens, d_middle, gain, others, **kw):
    count = d_mixed.shape[0]
    model = w_qkv.shape[0]

    n = len(others)

    def body(d, x, dm, g, *refs):
        rest, (w_in, out, packed, e, w, sems) = refs[:n], refs[n:]
        tiles = model // 256

        def copy(j):
            return pltpu.make_async_copy(w_in.at[j * 256 : (j + 1) * 256, :], w.at[j % 2], sems.at[j % 2])

        copy(0).start()
        for j in range(tiles):
            copy(j).wait()
            if j + 1 < tiles:
                copy(j + 1).start()
            e[:, j * 256 : (j + 1) * 256] = dot_nt(d[...], w[j % 2])

        def write(at, back):
            out[at] = dm[at] + back

        at = 0
        for part in (*norm_grad_rows(e, lambda at: x[at].astype(F32), g, count, write), *[r[...] for r in rest]):
            packed[:, at : at + part.shape[1]] = part
            at += part.shape[1]

    wide, size = (count, model), 2 * model + sum(o.shape[1] for o in others)
    return kernel_call(
        body, (), (d_mixed, tokens, d_middle, gain, *others), [(wide, F32, False), ((1, size), F32)], far=(w_qkv,),
        scratch=[
            pltpu.VMEM(wide, F32), pltpu.VMEM((2, 256, w_qkv.shape[1]), BF), pltpu.SemaphoreType.DMA((2,))
        ], limit=10, time=6.5, **kw,
    )


def layer_result(hidden, w_down, middle, down_bias, **kw):
    count, ff = hidden.shape
    model, tiles = w_down.shape[1], 8
    deep = ff // tiles

    def body(h, mid, b, w_in, out, w, total, sems):
        def copy(j):
            return pltpu.make_async_copy(w_in.at[j * deep : (j + 1) * deep, :], w.at[j % 3], sems.at[j % 3])

        copy(0).start()
        copy(1).start()
        for j in range(tiles):
            copy(j).wait()
            if j + 2 < tiles:
                copy(j + 2).start()
            part = dot(h[:, j * deep : (j + 1) * deep], w[j % 3])
            if j == 0:
                total[...] = mid[...] + b[...] + part
            elif j < tiles - 1:
                total[...] += part
            else:
                out[...] = (total[...] + part).astype(BF)

    return kernel_call(
        body, (), (hidden, middle, down_bias), [((count, model), BF, False)], far=(w_down,),
        scratch=[pltpu.VMEM((3, deep, model), BF), pltpu.VMEM((count, model), F32), pltpu.SemaphoreType.DMA((3,))],
        time=5.5, limit=9, **kw,
    )


def swap(v, pairs):
    return lax.ppermute(v, AXES, pairs)


def state_plan(doc_end, n_rows, n_seq, later=False):
    me = lax.axis_index("seq")

    def reaches(a, b):
        def at(i):
            return lax.dynamic_index_in_dim(doc_end, i, 1, keepdims=False)

        return (at(a) == at(b)).astype(F32)

    pairs, merges, coefs = [], [], []
    size = 1
    while size < n_seq:
        step = [(r * n_seq + s, r * n_seq + (s ^ size)) for r in range(n_rows) for s in range(n_seq)]
        if 2 * size == n_seq:
            step = [p for p in step if bool(p[0] % n_seq & size) == later]
        pairs.append(step)
        upper = (me // size) % 2 == 1
        low = me // (2 * size) * (2 * size)
        mid, high = low + size, low + 2 * size
        if later:
            coefs.append(jnp.where(upper, 0.0, reaches(me + 1, mid)))
            same = reaches(low, mid)
            merges.append(jnp.stack([jnp.where(upper, same, 1.0), jnp.where(upper, 1.0, same)]))
        else:
            coefs.append(jnp.where(upper, reaches(mid, me), 0.0))
            same = reaches(mid, high)
            merges.append(jnp.stack([jnp.where(upper, 1.0, same), jnp.where(upper, same, 1.0)]))
        size *= 2
    return pairs, merges, jnp.stack(coefs)


def stage_pairs(n_rows, n_seq):
    def pairs(bit0, bit1):
        return [(i, i ^ (bit1 if i & 1 else bit0)) for i in range(n_rows * n_seq)]

    return [pairs(2, 4), pairs(8, 8), pairs(4, 2), pairs(16, 16)]


def core_pairs(n):
    return [(i, i ^ 1) for i in range(n)]


def shard_tables(device):
    j = jnp.arange(32, dtype=jnp.int32)

    def bits(device):
        core = device & 1
        return jnp.where(core == 0, 1, 2), 3, jnp.where(core == 0, 2, 1), 4, 0

    def order(device):
        move = 0
        for k, at in enumerate(bits(device)):
            move = move | (((31 - j) >> (4 - k)) & 1) << at
        return device ^ move

    place = 0
    for k, at in enumerate(bits(device)):
        place = place | (1 - (((j ^ device) >> at) & 1)) << (4 - k)
    return jnp.stack([order(device), order(device ^ 1), place, jnp.broadcast_to(device & 1, (32,))])


def fold(parts, **kw):
    rows = parts[0][0].shape[0]
    widths = [k.shape[1] for k, g in parts]
    half, step, n = rows // 2, min(32, rows // 2), len(parts)

    def body(*refs):
        send, keep = refs[2 * n :]

        @pl.loop(0, half // step, unroll=min(2, half // step))
        def _(i):
            at = 0
            top, low = cut(i * step, step), cut(half + i * step, step)
            for k, w in enumerate(widths):
                a, b = refs[2 * k], refs[2 * k + 1]
                lanes = slice(at, at + w)
                send[top, lanes] = (a[top].astype(F32) + b[top].astype(F32)).astype(BF)
                keep[top, lanes] = a[low].astype(F32) + b[low].astype(F32)
                at += w

    shape = (half, sum(widths))
    return kernel_call(body, (), [x for p in parts for x in p], [(shape, BF), (shape, F32)], **kw)


def place(tables, pieces, side, **kw):
    rows = pieces[0][0].shape[0]

    def body(tables, *refs):
        core, out = tables[3, 0], refs[-1]
        for k, (mine, got, at, w, to) in enumerate(pieces):
            out[:, pl.ds(pl.multiple_of(core * side + to, 128), w)] = refs[2 * k][:, at : at + w]
            out[:, pl.ds(pl.multiple_of((1 - core) * side + to, 128), w)] = refs[2 * k + 1][:, at : at + w].astype(F32)

    args = [x for p in pieces for x in p[:2]]
    return kernel_call(body, (tables,), args, [((rows, 2 * side), F32, False)], **kw)


def settle(a, **kw):
    def body(a, out):
        out[...] = a[...]

    return kernel_call(body, (), (a,), [(a.shape, a.dtype)], **kw)


def add(a, b, **kw):
    def body(a, b, out):
        out[...] = a[...] + b[...]

    return kernel_call(body, (), (a, b), [(a.shape, a.dtype)], **kw)


def local(
    tokens, bounds, norm1_gain, norm1_bias, w_qkv, w_proj, norm2_gain, norm2_bias,
    w_up, up_bias, w_down, down_bias, cotangent, n_rows, n_seq,
):
    rows, span, model = tokens.shape
    ff = w_up.shape[1]
    count, n = rows * span, n_rows * n_seq
    seq = lax.axis_index("seq")
    device = lax.axis_index("rows") * n_seq + seq
    core = device & 1
    lb = bounds - seq * span
    ends = jnp.arange(n_seq + 1, dtype=jnp.int32) * span - 1
    doc_end = jnp.sum((bounds[:, None, :] <= ends[None, :, None]).astype(jnp.int32), -1)
    x, cot = tokens.reshape(count, model), cotangent.reshape(count, model)
    vectors = [v.reshape(1, -1) for v in (norm1_gain, norm1_bias, norm2_gain, norm2_bias, up_bias, down_bias)]
    shards = 32
    fast = n == shards and model % (shards * 32) == 0 and ff % (shards * 128) == 0
    tables = shard_tables(device)
    plan = state_plan(doc_end, n_rows, n_seq)
    back_plan = state_plan(doc_end, n_rows, n_seq, later=True)
    held, last, ran, beats = [], [], [], []

    def run(kernel, *args, **kw):
        used = {id(x) for x in jax.tree.leaves(args)}
        small = kernel in (fold, settle, add, merge_states, turned)
        beat = beats and len(ran) % BEAT == 0 and "small" not in state
        extra = beats[:] if beat else []
        kept = [] if small else [x for x in held if id(x) not in used]
        *outs, token = kernel(*args, hold=kept + last + extra, **kw)
        last[:] = [token]
        ran.append(kernel)
        if beat:
            beats[:] = [swap(token, core_pairs(n))]
        return outs[0] if len(outs) == 1 else outs

    def keep(*arrays):
        held.extend(arrays)

    def drop(*arrays):
        held[:] = [x for x in held if all(x is not y for y in arrays)]

    def merged(plan, gots, own):
        return run(merge_states, plan[1][len(gots) - 1], own, gots[-1])

    n1, km, v, own, *vectors = run(keys_values, lb, x, vectors, w_qkv, span)
    gain1, bias1, gain2, bias2, b_up, b_down = vectors
    keep(gain1, gain2, bias2, b_up, b_down)
    gots = [swap(own, plan[0][0])]
    qm, n1_t = run(queries, n1, w_qkv, tables, shards)
    group = own
    for pairs in plan[0][1:]:
        group = merged(plan, gots, group)
        gots.append(swap(group, pairs))
    numer, denom, wdown_v, wproj_v, cot_v = run(attend_inside, lb, qm, km, v, span, fetch=(w_down, w_proj, cot))
    drop(km, v, qm)
    keep(numer, denom, wproj_v, cot_v)
    d_act = run(active_grads, cot_v, wdown_v)
    keep(d_act)
    att, rden, middle, n2, wup_v = run(
        attend_join, lb, plan[2], gots, qm, numer, denom, x, wproj_v, gain2, bias2, span, fetch=(w_up,)
    )
    drop(numer, denom, wproj_v)
    keep(wup_v, n2)
    hidden, d_pre, g_up_bias = run(expand, n2, wup_v, b_up, d_act)
    drop(d_act)
    keep(hidden, d_pre)

    stages = [*stage_pairs(n_rows, n_seq), core_pairs(n)] if fast else []
    state = {}

    def other(name, kernel, *args):
        if fast:
            out = run(kernel, *args, tables)
            state[name] = (kernel, args, swap(out, core_pairs(n)))

    def mine(name):
        if fast:
            kernel, args, got = state[name]
            send, kept = run(kernel, *args, tables, got)
            state[name] = (kept, swap(send, stages[0]), 1)

    def step(name, *names):
        if fast:
            parts = [state[k] for k in names or (name,)]
            send, kept = run(fold, [p[:2] for p in parts])
            at = parts[0][2]
            state[name] = (kept, swap(send, stages[at]), at + 1)

    def end(to, side, *pieces):
        if fast:
            found = []
            for name, w, column, at in pieces:
                kept, got, unused = state[name]
                found.append((kept, got, at, w, column))
            grads[to] = run(place, tables, found, side)

    def arrived(name):
        if fast:
            kept, got, at = state[name]
            state[name] = (kept, run(settle, got), at)

    grads, small_step, box = {}, [0], {}
    half = ff // TILE // 2
    widths = [w * model // 2 // sum(DOWN) for w in DOWN]

    def small_sum():
        k = small_step[0]
        if k:
            state["small"] = run(add, state["small"], state["small got"])
        if k < 5:
            state["small got"] = swap(state["small"], [(i, i ^ (1 << k)) for i in range(n)])
        small_step[0] += 1

    def second_norm():
        box["d_mid"], box["branch"], *box["sums"], box["w_proj"] = run(
            second_norm_grads, d_pre, wup_v, middle, cot_v, gain2, fetch=(w_proj,)
        )

    def mixer():
        box["d_num"], box["d_den"], box["group"] = run(
            mixer_grads, lb, box["branch"], box["w_proj"], att, rden, qm, span
        )
        box["gots"] = [swap(box["group"], back_plan[0][0])]

    def merge():
        for pairs in back_plan[0][1:]:
            box["group"] = merged(back_plan, box["gots"], box["group"])
            box["gots"].append(swap(box["group"], pairs))

    def back():
        box["d_mixed"] = run(
            attend_back, lb, plan[2], back_plan[2], gots, box["gots"], qm, km, v,
            box["d_num"], box["d_den"], span,
        )

    def first_norm():
        g_gain2, g_bias2, g_down_bias = box["sums"]
        others = [g_gain2, g_bias2, g_up_bias, g_down_bias]
        box["grad_tokens"], state["small"] = run(
            first_norm_grads, box["d_mixed"], w_qkv, x, box["d_mid"], gain1, others
        )

    def layer():
        box["layer_out"] = run(layer_result, hidden, w_down, middle, b_down)

    def keep_as(name, *call):
        box[name] = run(*call)

    def down(k):
        return down_grad, box["hidden_t"], cot_v, widths[k], sum(widths[:k]), model // 2

    tasks = dict(
        dn2=second_norm, mixer=mixer, merge=merge, layer=layer, back=back, dn1=first_norm, small=small_sum,
        turn=lambda: keep_as("hidden_t", transposed, hidden),
        n2t=lambda: keep_as("n2_t", turned, n2, tables, shards),
        att=lambda: keep_as("att_t", turned, att, tables, shards),
        d1o=lambda: other("d1", *down(0)),
        d2o=lambda: other("d2", *down(1)),
        uo=lambda: other("u", weight_grad, box["n2_t"], d_pre, 0, half, half),
        po=lambda: other("p", weight_grad, box["att_t"], box["branch"], 0, 1, 1),
        q1o=lambda: other("q1", weight_grad, n1_t, box["d_mixed"], 0, 2, 3),
        q2o=lambda: other("q2", weight_grad, n1_t, box["d_mixed"], 2, 1, 3),
        d1a=lambda: arrived("d1"),
        de=lambda: end("down", model // 2, ("d1", widths[0], 0, 0), ("d2", widths[1], widths[0], 0)),
        ue=lambda: end("up", ff // 2, ("u", ff // 2, 0, 0)),
        pe=lambda: end("proj", model // 2, ("p", TILE, 0, 0)),
        qe=lambda: end("qkv", 3 * TILE, ("q1", 2 * TILE, 0, 0), ("q2", TILE, 2 * TILE, 0)),
    )
    for name in ("d1", "d2", "u", "p", "q1", "q2"):
        tasks[name + "m"] = functools.partial(mine, name)
        tasks[name + "f"] = functools.partial(step, name)
    pinned = dict(
        hidden=(lambda: hidden, ("turn",)), d_pre=(lambda: d_pre, ("uo", "um", "dn2",)), cot=(lambda: cot_v, ("d1o", "d2o", "d1m", "d2m", "dn2",)),
        w_up=(lambda: wup_v, ("dn2",)), n2=(lambda: n2, ("n2t",)), hidden_t=(lambda: box.get("hidden_t"), ("d1o", "d2o", "d1m", "d2m",)),
        w_proj=(lambda: box.get("w_proj"), ("mixer",)),
        d_mixed=(lambda: box.get("d_mixed"), ("q1o", "q2o", "q1m", "q2m", "dn1",)), gain2=(lambda: gain2, ("dn2",)), b_down=(lambda: b_down, ("layer",)),
        gain1=(lambda: gain1, ("dn1",)),
    )
    local_steps = ("dn2", "mixer", "merge", "layer", "back", "dn1")
    steps = [name for name in STEPS if fast or name in local_steps]
    if fast:
        beats[:] = [swap(last[0], core_pairs(n))]
    for k, name in enumerate(steps):
        later = set(steps[k:])
        held[:] = [a for a in (get() for get, uses in pinned.values() if later & set(uses)) if a is not None]
        tasks[name]()
    d_mixed, branch = box["d_mixed"], box["branch"]
    layer_out, grad_tokens, small = box["layer_out"], box["grad_tokens"], state["small"]
    sizes = [model, model, model, model, ff, model]
    if fast:
        cuts, at = [], 0
        for size in sizes:
            cuts.append(lax.dynamic_slice(state["small"], (0, at + device * (size // n)), (1, size // n)).reshape(size // n))
            at += size
    else:
        scatter = lambda g: lax.psum_scatter(g, AXES, scatter_dimension=0, tiled=True)
        factors = dict(qkv=(n1, d_mixed), proj=(att, branch), up=(n2, d_pre), down=(hidden, cot))
        grads = {k: scatter(dot_tn(*ab)) for k, ab in factors.items()}
        cuts, at = [], 0
        for size in sizes:
            cuts.append(scatter(small[0, at : at + size]))
            at += size
    shape = (rows, span, model)
    return (
        layer_out.reshape(shape), grad_tokens.reshape(shape), cuts[0], cuts[1], grads["qkv"], grads["proj"],
        cuts[2], cuts[3], grads["up"], cuts[4], grads["down"], cuts[5],
    )


def solution(mesh):
    wide, row, whole = P("rows", "seq", None), P(AXES), P()
    in_specs = (wide, P("rows", None), *[whole] * 10, wide)
    out_specs = (wide, wide, *[row] * 10)
    body = functools.partial(local, n_rows=mesh.shape["rows"], n_seq=mesh.shape["seq"])
    return jax.shard_map(body, mesh=mesh, in_specs=in_specs, out_specs=out_specs, check_vma=False)
```

profile of v0, /device:TPU:0, one launch (start us, length us, event | category | flops | bytes accessed | tf_op | source)
XLA Modules:
  0.0 220.8 jit_solution(3968169727285727583)
XLA Ops:
  1.3 6.5 %keys_values.1 = (bf16[512,1024]{1,0:T(8,128)(2,1)S(1)}, bf16[512,1024]{1,0:T(8,128)(2,1)S(1)}, bf16[512,1024]{1,0:T(8,128)(2,1)S(1)}, bf16[2,8,80,128]{3,2,1,0:...) custom-call(s32[2,4]{1,0:T(2,128)S(1)} %broadcast_subtract_fusion.re, ...), custom_call_target="tpu_custom_call" | custom-call | flops 73000001536 | bytes 1 | tf_op jit(solution)/shard_map/keys_values/pallas_call | solution.py:79
  9.8 3.7 %queries.1 = (bf16[512,1024]{1,0:T(8,128)(2,1)S(1)}, bf16[1024,512]{1,0:T(8,128)(2,1)S(1)}, f32[8,128]{1,0:T(8,128)S(1)}) custom-call(s32[4,32]{1,0:T(4,128)S(1)} %add_add_fusion.refs_0_, bf16[512,1024]{1,0:T(8,128)(2,1)S(1)} %get-tuple-element.193.refs_1_, bf16[1024,3072]{1,0:T(8,128)(2,1)} %refs_8_.3, ...), custom_call_target="tpu_custom_call" | custom-call | flops 38999998464 | bytes 1 | tf_op jit(solution)/shard_map/queries/pallas_call | solution.py:79
  14.3 5.0 %collective-permute-start.1 = (bf16[2,8,80,128]{3,2,1,0:T(8,128)(2,1)S(1)}, bf16[2,8,80,128]{3,2,1,0:T(8,128)(2,1)S(1)}, u32[]{:S(2)}, u32[]{:S(2)}) collective-permute-start(bf16[2,8,80,128]{3,2,1,0:T(8,128)(2,1)S(1)} %get-tuple-element.201), channel_id=1, source_target_pairs={{0,2},{1,3},{4,6},{5,7},{8,10},{9,11},{12,14},{13,15},{16,18},{17,... | collective-permute-start | bytes 983048 | tf_op jit(solution)/shard_map/ppermute | solution.py:686
  19.4 4.8 %attend_inside.1 = (f32[512,1024]{1,0:T(8,128)S(1)}, f32[512,1024]{1,0:T(8,128)S(1)}, bf16[4096,1024]{1,0:T(8,128)(2,1)S(1)}, bf16[1024,1024]{1,0:T(8,128)(2,1)S...) custom-call(s32[2,4]{1,0:T(2,128)S(1)} %broadcast_subtract_fusion.refs_0_, ...), custom_call_target="tpu_custom_call" | custom-call | flops 57000001536 | bytes 1 | tf_op jit(solution)/shard_map/attend_inside/pallas_call | solution.py:79
  24.2 4.6 %active_grads.1 = (bf16[512,4096]{1,0:T(8,128)(2,1)S(1)}, f32[8,128]{1,0:T(8,128)S(1)}) custom-call(bf16[512,1024]{1,0:T(8,128)(2,1)S(1)} %get-tuple-element.209.refs_0_.refs_14_.refs_8_.refs_2_.refs_3_, bf16[4096,1024]{1,0:T(8,128)(2,1)S(1)} %get-tuple-element.210.refs_1_, ...), custom_call_target="tpu_custom_call" | custom-call | flops 44999999488 | bytes 1 | tf_op jit(solution)/shard_map/active_grads/pallas_call | solution.py:79
  28.8 4.4 %attend_join.1 = (bf16[512,1024]{1,0:T(8,128)(2,1)S(1)}, f32[512,1024]{1,0:T(8,128)S(1)}, f32[512,1024]{1,0:T(8,128)S(1)}, bf16[512,1024]{1,0:T(8,128)(2,1)S(1)}...) custom-call(s32[2,4]{1,0:T(2,128)S(1)} %broadcast_subtract_fusion.refs_0_, f32[2,2]{1,0:T(2,128)S(1)} %pad_maximum_fusion.refs_1_, ...), custom_call_target="tpu_custom_call" | custom-call | flops 49999998976 | bytes 1 | tf_op jit(solution)/shard_map/attend_join/pallas_call | solution.py:79
  33.2 10.3 %expand.1 = (bf16[512,4096]{1,0:T(8,128)(2,1)S(1)}, bf16[512,4096]{1,0:T(8,128)(2,1)S(1)}, f32[1,4096]{1,0:T(1,128)S(1)}, f32[8,128]{1,0:T(8,128)S(1)}) custom-call(bf16[512,1024]{1,0:T(8,128)(2,1)S(1)} %get-tuple-element.214.refs_0_.refs_4_.refs_5_.refs_6_.refs_1_, bf16[1024,4096]{1,0:T(8,128)(2,1)S(1)} %get-tuple-element.215.refs_1_.refs_3_.refs_4_.refs_5_, ...), custom_call_target="tpu_custom_call" | custom-call | flops 109999996928 | bytes 1 | tf_op jit(solution)/shard_map/expand/pallas_call | solution.py:79
  45.6 1.8 down_grad.4
  47.6 2.9 %down_grad.5 = (bf16[4096,384]{1,0:T(8,128)(2,1)S(1)}, f32[8,128]{1,0:T(8,128)S(1)}) custom-call(s32[4,32]{1,0:T(4,128)S(1)} %copy-done.1, bf16[4096,512]{1,0:T(8,128)(2,1)S(1)} %get-tuple-element.221.refs_1_.refs_6_, bf16[512,1024]{1,0:T(8,128)(2,1)S(1)} %get-tuple-element.209.refs_0_.refs_14_.refs_8_.refs_2_.refs_3_, ...), custom_call_target="tpu_custom_call" | custom-call | flops 34909089792 | bytes 1 | tf_op jit(solution)/shard_map/down_grad/pallas_call | solution.py:79
  51.2 2.3 %down_grad.6 = (bf16[2048,128]{1,0:T(8,128)(2,1)}, bf16[2048,128]{1,0:T(8,128)(2,1)S(1)}, f32[8,128]{1,0:T(8,128)S(1)}) custom-call(s32[4,32]{1,0:T(4,128)S(1)} %copy-done.1, bf16[4096,512]{1,0:T(8,128)(2,1)S(1)} %get-tuple-element.221.refs_1_.refs_6_, bf16[512,1024]{1,0:T(8,128)(2,1)S(1)} %get-tuple-element.209.refs_0_.refs_14_.refs_8_.refs_2_.refs_3_, ...), custom_call_target="tpu_custom_call" | custom-call | flops 11636363264 | bytes 1 | tf_op jit(solution)/shard_map/down_grad/pallas_call | solution.py:79
  53.4 6.7 %second_norm_grads.1 = (f32[512,1024]{1,0:T(8,128)S(1)}, bf16[512,1024]{1,0:T(8,128)(2,1)S(1)}, f32[1,1024]{1,0:T(1,128)S(1)}, f32[1,1024]{1,0:T(1,128)S(1)}, f3...) custom-call(bf16[512,4096]{1,0:T(8,128)(2,1)S(1)} %get-tuple-element.219.refs_1_.refs_3_.refs_4_.refs_0_.re, ...), custom_call_target="tpu_custom_call" | custom-call | flops 70000001024 | bytes 1 | tf_op jit(solution)/shard_map/second_norm_grads/pallas_call | solution.py:79
  60.2 4.1 %down_grad.7 = (bf16[2048,384]{1,0:T(8,128)(2,1)}, bf16[2048,384]{1,0:T(8,128)(2,1)S(1)}, f32[8,128]{1,0:T(8,128)S(1)}) custom-call(s32[4,32]{1,0:T(4,128)S(1)} %copy-done.1, bf16[4096,512]{1,0:T(8,128)(2,1)S(1)} %get-tuple-element.221.refs_1_.refs_6_, bf16[512,1024]{1,0:T(8,128)(2,1)S(1)} %get-tuple-element.209.refs_0_.refs_14_.refs_8_.refs_2_.refs_3_, ...), custom_call_target="tpu_custom_call" | custom-call | flops 34909089792 | bytes 1 | tf_op jit(solution)/shard_map/down_grad/pallas_call | solution.py:79
  65.2 1.7 collective-permute-start.8
  66.8 2.9 %weight_grad.8 = (bf16[1024,2048]{1,0:T(8,128)(2,1)S(1)}, f32[8,128]{1,0:T(8,128)S(1)}) custom-call(s32[4,32]{1,0:T(4,128)S(1)} %copy-done.1, bf16[1024,512]{1,0:T(8,128)(2,1)S(1)} %get-tuple-element.231.refs_1_, bf16[512,4096]{1,0:T(8,128)(2,1)S(1)} %get-tuple-element.219.refs_1_.refs_3_.refs_4_.refs_0_.refs_2_.refs_6_, ...), custom_call_target="tpu_custom_call" | custom-call | flops 35999997952 | bytes 1 | tf_op jit(solution)/shard_map/weight_grad/pallas_call | solution.py:79
  72.1 1.6 collective-permute-start.10
  73.8 4.3 %mixer_grads.1 = (bf16[512,1024]{1,0:T(8,128)(2,1)S(1)}, f32[512,1024]{1,0:T(8,128)S(1)}, bf16[2,8,80,128]{3,2,1,0:T(8,128)(2,1)S(1)}, f32[8,128]{1,0:T(8,128)S(1)}) custom-call(s32[2,4]{1,0:T(2,128)S(1)} %broadcast_subtract_fusion.refs_0_, bf16[512,1024]{1,0:T(8,128)(2,1)S(1)} %get-tuple-element.234.refs_1_.refs_2_, ...), custom_call_target="tpu_custom_call" | custom-call | flops 49999998976 | bytes 1 | tf_op jit(solution)/shard_map/mixer_grads/pallas_call | solution.py:79
  78.6 1.6 collective-permute-done.10.refs_1_
  80.3 1.6 collective-permute-start.13
  83.9 4.1 %weight_grad.9 = (bf16[512,2048]{1,0:T(8,128)(2,1)}, bf16[512,2048]{1,0:T(8,128)(2,1)S(1)}, f32[8,128]{1,0:T(8,128)S(1)}) custom-call(s32[4,32]{1,0:T(4,128)S(1)} %copy-done.1, bf16[1024,512]{1,0:T(8,128)(2,1)S(1)} %get-tuple-element.231.refs_1_, bf16[512,4096]{1,0:T(8,128)(2,1)S(1)} %get-tuple-element.219.refs_1_.refs_3_.refs_4_.refs_0_.refs_2_.refs_6_, ...), custom_call_target="tpu_custom_call" | custom-call | flops 35999997952 | bytes 1 | tf_op jit(solution)/shard_map/weight_grad/pallas_call | solution.py:79
  88.0 7.6 %layer_result.1 = (bf16[512,1024]{1,0:T(8,128)(2,1)}, f32[8,128]{1,0:T(8,128)S(1)}) custom-call(bf16[512,4096]{1,0:T(8,128)(2,1)S(1)} %copy-done.10, f32[512,1024]{1,0:T(8,128)S(1)} %copy-done.12, f32[1,1024]{1,0:T(1,128)S(1)} %get-tuple-element.198.refs_7_.refs_8_.refs_6_.refs_13_.refs_4_.refs_2_, bf16[4096,1024]{1,0:T(8,128)(2,1)} %refs_3_.1, ...), custom_call_target="tpu_custom_call" | custom-call | flops 54999998464 | bytes 1 | tf_op jit(solution)/shard_map/layer_result/pallas_call | solution.py:79
  95.6 3.1 %fold.26 = (bf16[1024,384]{1,0:T(8,128)(2,1)}, f32[1024,384]{1,0:T(8,128)S(1)}, f32[8,128]{1,0:T(8,128)S(1)}) custom-call(bf16[2048,384]{1,0:T(8,128)(2,1)S(1)} %get-tuple-element.254.refs_0_, bf16[2048,384]{1,0:T(8,128)(2,1)} %collective-permute-done.14.refs_1_, f32[8,128]{1,0:T(8,128)S(1)} %get-tuple-element.256.refs_2_, ...), custom_call_target="tpu_custom_call" | custom-call | flops 5000000000 | bytes 1 | tf_op jit(solution)/shard_map/fold/pallas_call | solution.py:79
  99.3 2.7 %collective-permute-start.18 = (bf16[512,2048]{1,0:T(8,128)(2,1)}, bf16[512,2048]{1,0:T(8,128)(2,1)}, u32[]{:S(2)}, u32[]{:S(2)}) collective-permute-start(bf16[512,2048]{1,0:T(8,128)(2,1)} %get-tuple-element.271), channel_id=1, source_target_pairs={{0,2},{1,5},{2,0},{3,7},{4,6},{5,1},{6,4},{7,3},{8,10},{9,13},{10,... | collective-permute-start | bytes 6291464 | tf_op jit(solution)/shard_map/ppermute | solution.py:686
  101.9 1.6 collective-permute-start.21
  105.2 10.3 %attend_back.1 = (bf16[512,3072]{1,0:T(8,128)(2,1)S(1)}, f32[8,128]{1,0:T(8,128)S(1)}) custom-call(s32[2,4]{1,0:T(2,128)S(1)} %broadcast_subtract_fusion.refs_0_, f32[2,2]{1,0:T(2,128)S(1)} %pad_maximum_fusion.refs_1_, f32[2,2]{1,0:T(2,128)S(1)} %pad_maximum_fusion.3.refs_2_, bf16[2,8,80,128]{3,2,1,0:T(8,128)(2,1)S(1)} %collective-permute-done.refs_2_.refs_3_, ...), custom_call_target="tpu_custom_call" | custom-call | flops 120000004096 | bytes 1 | tf_op jit(solution)/shard_map/attend_back/pallas_call | solution.py:79
  116.3 1.8 weight_grad.10
  118.3 2.7 %collective-permute-start.19 = (bf16[256,128]{1,0:T(8,128)(2,1)S(1)}, bf16[256,128]{1,0:T(8,128)(2,1)S(1)}, u32[]{:S(2)}, u32[]{:S(2)}) collective-permute-start(bf16[256,128]{1,0:T(8,128)(2,1)S(1)} %get-tuple-element.273), channel_id=1, source_target_pairs={{0,16},{1,17},{2,18},{3,19},{4,20},{5,21},{6,22},{7,23},{8,24},{9,... | collective-permute-start | bytes 196616 | tf_op jit(solution)/shard_map/ppermute | solution.py:686
  121.1 3.9 %collective-permute-done.19.refs_1_ = bf16[256,128]{1,0:T(8,128)(2,1)S(1)} collective-permute-done((bf16[256,128]{1,0:T(8,128)(2,1)S(1)}, bf16[256,128]{1,0:T(8,128)(2,1)S(1)}, u32[]{:S(2)}, u32[]{:S(2)}) %collective-permute-start.19) | collective-permute-done | bytes 65568 | tf_op jit(solution)/shard_map/ppermute | solution.py:686
  127.6 2.1 fold.30
  130.0 1.8 weight_grad.11
  135.1 1.9 collective-permute-start.30
  137.0 1.8 collective-permute-start.33
  141.5 11.7 %first_norm_grads.1 = (f32[512,1024]{1,0:T(8,128)}, f32[1,9216]{1,0:T(1,128)S(1)}, f32[8,128]{1,0:T(8,128)S(1)}) custom-call(bf16[512,3072]{1,0:T(8,128)(2,1)S(1)} %get-tuple-element.259.refs_2_.refs_3_.refs_4_.refs_0_, bf16[512,1024]{1,0:T(8,128)(2,1)S(1)} %bitcast.33, f32[512,1024]{1,0:T(8,128)S(1)} %get-tuple-element.260.refs_2_, ...), custom_call_target="tpu_custom_call" | custom-call | flops 65000001536 | bytes 1 | tf_op jit(solution)/shard_map/first_norm_grads/pallas_call | solution.py:79
  155.3 1.4 collective-permute-done.30.refs_1_
  156.8 1.5 collective-permute-start.35
  158.6 3.7 %collective-permute-start.40 = (bf16[256,1024]{1,0:T(8,128)(2,1)S(1)}, bf16[256,1024]{1,0:T(8,128)(2,1)S(1)}, u32[]{:S(2)}, u32[]{:S(2)}) collective-permute-start(bf16[256,1024]{1,0:T(8,128)(2,1)S(1)} %get-tuple-element.327), channel_id=1, source_target_pairs={{0,8},{1,9},{2,10},{3,11},{4,12},{5,13},{6,14},{7,15},{8,0},{9,1},... | collective-permute-start | bytes 1572872 | tf_op jit(solution)/shard_map/ppermute | solution.py:686
  162.3 1.4 place.4
  165.5 5.9 %collective-permute-done.35.refs_1_ = bf16[512,512]{1,0:T(8,128)(2,1)S(1)} collective-permute-done((bf16[512,512]{1,0:T(8,128)(2,1)S(1)}, bf16[512,512]{1,0:T(8,128)(2,1)S(1)}, u32[]{:S(2)}, u32[]{:S(2)}) %collective-permute-start.35) | collective-permute-done | bytes 524320 | tf_op jit(solution)/shard_map/ppermute | solution.py:686
  171.6 1.5 collective-permute-start.42
  174.7 11.7 %collective-permute-done.37.refs_1_ = bf16[256,512]{1,0:T(8,128)(2,1)S(1)} collective-permute-done((bf16[256,512]{1,0:T(8,128)(2,1)S(1)}, bf16[256,512]{1,0:T(8,128)(2,1)S(1)}, u32[]{:S(2)}, u32[]{:S(2)}) %collective-permute-start.37) | collective-permute-done | bytes 262176 | tf_op jit(solution)/shard_map/ppermute | solution.py:686
  187.2 1.6 collective-permute-start.44
  188.8 2.6 %collective-permute-done.39.refs_1_ = f32[1,9216]{1,0:T(1,128)S(1)} collective-permute-done((f32[1,9216]{1,0:T(1,128)S(1)}, f32[1,9216]{1,0:T(1,128)S(1)}, u32[]{:S(2)}, u32[]{:S(2)}) %collective-permute-start.39) | collective-permute-done | bytes 36896 | tf_op jit(solution)/shard_map/ppermute | solution.py:686
  191.4 1.8 collective-permute-start.41
  194.4 1.8 collective-permute-done.41.refs_1_
  196.4 2.0 collective-permute-done.46.refs_1_
  199.9 1.4 place.5
  201.3 3.8 %collective-permute-done.48.refs_1_ = bf16[64,512]{1,0:T(8,128)(2,1)S(1)} collective-permute-done((bf16[64,512]{1,0:T(8,128)(2,1)S(1)}, bf16[64,512]{1,0:T(8,128)(2,1)S(1)}, u32[]{:S(2)}, u32[]{:S(2)}) %collective-permute-start.48) | collective-permute-done | bytes 65568 | tf_op jit(solution)/shard_map/ppermute | solution.py:686
  205.8 2.9 %collective-permute-start.47 = (bf16[64,512]{1,0:T(8,128)(2,1)S(1)}, bf16[64,512]{1,0:T(8,128)(2,1)S(1)}, u32[]{:S(2)}, u32[]{:S(2)}) collective-permute-start(bf16[64,512]{1,0:T(8,128)(2,1)S(1)} %get-tuple-element.348), channel_id=1, source_target_pairs={{0,16},{1,17},{2,18},{3,19},{4,20},{5,21},{6,22},{7,23},{8,24},{9,... | collective-permute-start | bytes 196616 | tf_op jit(solution)/shard_map/ppermute | solution.py:686
  210.0 7.8 %collective-permute-done.47.refs_1_ = bf16[64,512]{1,0:T(8,128)(2,1)S(1)} collective-permute-done((bf16[64,512]{1,0:T(8,128)(2,1)S(1)}, bf16[64,512]{1,0:T(8,128)(2,1)S(1)}, u32[]{:S(2)}, u32[]{:S(2)}) %collective-permute-start.47) | collective-permute-done | bytes 65568 | tf_op jit(solution)/shard_map/ppermute | solution.py:686
  (178 shorter events, 38.6 us)
Async XLA Ops:
  8.8 4.8 %collective-permute-start = (bf16[2,8,80,128]{3,2,1,0:T(8,128)(2,1)S(1)}, bf16[2,8,80,128]{3,2,1,0:T(8,128)(2,1)S(1)}, u32[]{:S(2)}, u32[]{:S(2)}) collective-permute-start(bf16[2,8,80,128]{3,2,1,0:T(8,128)(2,1)S(1)} %get-tuple-element.192.refs_1_), channel_id=1, source_target_pairs={{0,1},{1,0},{2,3},{3,2},{4,5},{5,4},{6,7},{7,6},{8,9},{9,8},{10,11... | collective-permute-start | bytes 983048 | tf_op jit(solution)/shard_map/ppermute | solution.py:686
  14.3 14.5 %collective-permute-start.1 = (bf16[2,8,80,128]{3,2,1,0:T(8,128)(2,1)S(1)}, bf16[2,8,80,128]{3,2,1,0:T(8,128)(2,1)S(1)}, u32[]{:S(2)}, u32[]{:S(2)}) collective-permute-start(bf16[2,8,80,128]{3,2,1,0:T(8,128)(2,1)S(1)} %get-tuple-element.201), channel_id=1, source_target_pairs={{0,2},{1,3},{4,6},{5,7},{8,10},{9,11},{12,14},{13,15},{16,18},{17,... | collective-permute-start | bytes 983048 | tf_op jit(solution)/shard_map/ppermute | solution.py:686
  43.5 4.1 %collective-permute-start.2 = (f32[8,128]{1,0:T(8,128)S(1)}, f32[8,128]{1,0:T(8,128)S(1)}, u32[]{:S(2)}, u32[]{:S(2)}) collective-permute-start(f32[8,128]{1,0:T(8,128)S(1)} %get-tuple-element.220.refs_8_), channel_id=1, source_target_pairs={{0,1},{1,0},{2,3},{3,2},{4,5},{5,4},{6,7},{7,6},{8,9},{9,8},{10,11... | collective-permute-start | bytes 12296 | tf_op jit(solution)/shard_map/ppermute | solution.py:686
  47.4 3.7 %collective-permute-start.4 = (bf16[4096,128]{1,0:T(8,128)(2,1)S(1)}, bf16[4096,128]{1,0:T(8,128)(2,1)S(1)}, u32[]{:S(2)}, u32[]{:S(2)}) collective-permute-start(bf16[4096,128]{1,0:T(8,128)(2,1)S(1)} %get-tuple-element.225), channel_id=1, source_target_pairs={{0,1},{1,0},{2,3},{3,2},{4,5},{5,4},{6,7},{7,6},{8,9},{9,8},{10,11... | collective-permute-start | bytes 3145736 | tf_op jit(solution)/shard_map/ppermute | solution.py:686
  50.6 9.6 %collective-permute-start.3 = (bf16[4096,384]{1,0:T(8,128)(2,1)S(1)}, bf16[4096,384]{1,0:T(8,128)(2,1)S(1)}, u32[]{:S(2)}, u32[]{:S(2)}) collective-permute-start(bf16[4096,384]{1,0:T(8,128)(2,1)S(1)} %get-tuple-element.224), channel_id=1, source_target_pairs={{0,1},{1,0},{2,3},{3,2},{4,5},{5,4},{6,7},{7,6},{8,9},{9,8},{10,11... | collective-permute-start | bytes 9437192 | tf_op jit(solution)/shard_map/ppermute | solution.py:686
  51.0 9.2 %collective-permute-start.5 = (f32[8,128]{1,0:T(8,128)S(1)}, f32[8,128]{1,0:T(8,128)S(1)}, u32[]{:S(2)}, u32[]{:S(2)}) collective-permute-start(f32[8,128]{1,0:T(8,128)S(1)} %get-tuple-element.226.refs_10_), channel_id=1, source_target_pairs={{0,1},{1,0},{2,3},{3,2},{4,5},{5,4},{6,7},{7,6},{8,9},{9,8},{10,11... | collective-permute-start | bytes 12296 | tf_op jit(solution)/shard_map/ppermute | solution.py:686
  53.4 17.3 %collective-permute-start.7 = (bf16[2048,128]{1,0:T(8,128)(2,1)}, bf16[2048,128]{1,0:T(8,128)(2,1)}, u32[]{:S(2)}, u32[]{:S(2)}) collective-permute-start(bf16[2048,128]{1,0:T(8,128)(2,1)} %get-tuple-element.238), channel_id=1, source_target_pairs={{0,2},{1,5},{2,0},{3,7},{4,6},{5,1},{6,4},{7,3},{8,10},{9,13},{10,... | collective-permute-start | bytes 1572872 | tf_op jit(solution)/shard_map/ppermute | solution.py:686
  65.2 5.6 %collective-permute-start.8 = (f32[8,128]{1,0:T(8,128)S(1)}, f32[8,128]{1,0:T(8,128)S(1)}, u32[]{:S(2)}, u32[]{:S(2)}) collective-permute-start(f32[8,128]{1,0:T(8,128)S(1)} %get-tuple-element.230.refs_2_), channel_id=1, source_target_pairs={{0,1},{1,0},{2,3},{3,2},{4,5},{5,4},{6,7},{7,6},{8,9},{9,8},{10,11... | collective-permute-start | bytes 12296 | tf_op jit(solution)/shard_map/ppermute | solution.py:686
  69.7 14.2 %collective-permute-start.6 = (bf16[1024,2048]{1,0:T(8,128)(2,1)S(1)}, bf16[1024,2048]{1,0:T(8,128)(2,1)S(1)}, u32[]{:S(2)}, u32[]{:S(2)}) collective-permute-start(bf16[1024,2048]{1,0:T(8,128)(2,1)S(1)} %get-tuple-element.233), channel_id=1, source_target_pairs={{0,1},{1,0},{2,3},{3,2},{4,5},{5,4},{6,7},{7,6},{8,9},{9,8},{10,11... | collective-permute-start | bytes 12582920 | tf_op jit(solution)/shard_map/ppermute | solution.py:686
  69.8 25.8 %collective-permute-start.14 = (bf16[2048,384]{1,0:T(8,128)(2,1)}, bf16[2048,384]{1,0:T(8,128)(2,1)}, u32[]{:S(2)}, u32[]{:S(2)}) collective-permute-start(bf16[2048,384]{1,0:T(8,128)(2,1)} %get-tuple-element.255), channel_id=1, source_target_pairs={{0,2},{1,5},{2,0},{3,7},{4,6},{5,1},{6,4},{7,3},{8,10},{9,13},{10,... | collective-permute-start | bytes 4718600 | tf_op jit(solution)/shard_map/ppermute | solution.py:686
  72.1 8.1 %collective-permute-start.10 = (bf16[1024,128]{1,0:T(8,128)(2,1)S(1)}, bf16[1024,128]{1,0:T(8,128)(2,1)S(1)}, u32[]{:S(2)}, u32[]{:S(2)}) collective-permute-start(bf16[1024,128]{1,0:T(8,128)(2,1)S(1)} %get-tuple-element.243), channel_id=1, source_target_pairs={{0,8},{1,9},{2,10},{3,11},{4,12},{5,13},{6,14},{7,15},{8,0},{9,1},... | collective-permute-start | bytes 786440 | tf_op jit(solution)/shard_map/ppermute | solution.py:686
  73.7 8.1 %collective-permute-start.11 = (f32[8,128]{1,0:T(8,128)S(1)}, f32[8,128]{1,0:T(8,128)S(1)}, u32[]{:S(2)}, u32[]{:S(2)}) collective-permute-start(f32[8,128]{1,0:T(8,128)S(1)} %get-tuple-element.240.refs_9_), channel_id=1, source_target_pairs={{0,1},{1,0},{2,3},{3,2},{4,5},{5,4},{6,7},{7,6},{8,9},{9,8},{10,11... | collective-permute-start | bytes 12296 | tf_op jit(solution)/shard_map/ppermute | solution.py:686
  78.0 3.8 %collective-permute-start.9 = (bf16[2,8,80,128]{3,2,1,0:T(8,128)(2,1)S(1)}, bf16[2,8,80,128]{3,2,1,0:T(8,128)(2,1)S(1)}, u32[]{:S(2)}, u32[]{:S(2)}) collective-permute-start(bf16[2,8,80,128]{3,2,1,0:T(8,128)(2,1)S(1)} %get-tuple-element.241.refs_1_), channel_id=1, source_target_pairs={{0,1},{1,0},{2,3},{3,2},{4,5},{5,4},{6,7},{7,6},{8,9},{9,8},{10,11... | collective-permute-start | bytes 983048 | tf_op jit(solution)/shard_map/ppermute | solution.py:686
  80.3 23.3 %collective-permute-start.13 = (bf16[512,128]{1,0:T(8,128)(2,1)S(1)}, bf16[512,128]{1,0:T(8,128)(2,1)S(1)}, u32[]{:S(2)}, u32[]{:S(2)}) collective-permute-start(bf16[512,128]{1,0:T(8,128)(2,1)S(1)} %get-tuple-element.253), channel_id=1, source_target_pairs={{0,4},{1,3},{2,6},{3,1},{4,0},{5,7},{6,2},{7,5},{8,12},{9,11},{10,... | collective-permute-start | bytes 393224 | tf_op jit(solution)/shard_map/ppermute | solution.py:686
  82.5 21.1 %collective-permute-start.12 = (bf16[2,8,80,128]{3,2,1,0:T(8,128)(2,1)S(1)}, bf16[2,8,80,128]{3,2,1,0:T(8,128)(2,1)S(1)}, u32[]{:S(2)}, u32[]{:S(2)}) collective-permute-start(bf16[2,8,80,128]{3,2,1,0:T(8,128)(2,1)S(1)} %get-tuple-element.249), channel_id=1, source_target_pairs={{2,0},{3,1},{6,4},{7,5},{10,8},{11,9},{14,12},{15,13},{18,16},{19,... | collective-permute-start | bytes 983048 | tf_op jit(solution)/shard_map/ppermute | solution.py:686
  83.8 11.8 %collective-permute-start.15 = (f32[8,128]{1,0:T(8,128)S(1)}, f32[8,128]{1,0:T(8,128)S(1)}, u32[]{:S(2)}, u32[]{:S(2)}) collective-permute-start(f32[8,128]{1,0:T(8,128)S(1)} %get-tuple-element.246.refs_6_), channel_id=1, source_target_pairs={{0,1},{1,0},{2,3},{3,2},{4,5},{5,4},{6,7},{7,6},{8,9},{9,8},{10,11... | collective-permute-start | bytes 12296 | tf_op jit(solution)/shard_map/ppermute | solution.py:686
  98.8 16.7 %collective-permute-start.16 = (f32[8,128]{1,0:T(8,128)S(1)}, f32[8,128]{1,0:T(8,128)S(1)}, u32[]{:S(2)}, u32[]{:S(2)}) collective-permute-start(f32[8,128]{1,0:T(8,128)S(1)} %get-tuple-element.257.refs_2_), channel_id=1, source_target_pairs={{0,1},{1,0},{2,3},{3,2},{4,5},{5,4},{6,7},{7,6},{8,9},{9,8},{10,11... | collective-permute-start | bytes 12296 | tf_op jit(solution)/shard_map/ppermute | solution.py:686
  99.3 28.3 %collective-permute-start.18 = (bf16[512,2048]{1,0:T(8,128)(2,1)}, bf16[512,2048]{1,0:T(8,128)(2,1)}, u32[]{:S(2)}, u32[]{:S(2)}) collective-permute-start(bf16[512,2048]{1,0:T(8,128)(2,1)} %get-tuple-element.271), channel_id=1, source_target_pairs={{0,2},{1,5},{2,0},{3,7},{4,6},{5,1},{6,4},{7,3},{8,10},{9,13},{10,... | collective-permute-start | bytes 6291464 | tf_op jit(solution)/shard_map/ppermute | solution.py:686
  101.9 23.2 %collective-permute-start.21 = (bf16[1024,384]{1,0:T(8,128)(2,1)}, bf16[1024,384]{1,0:T(8,128)(2,1)}, u32[]{:S(2)}, u32[]{:S(2)}) collective-permute-start(bf16[1024,384]{1,0:T(8,128)(2,1)} %get-tuple-element.277), channel_id=1, source_target_pairs={{0,8},{1,9},{2,10},{3,11},{4,12},{5,13},{6,14},{7,15},{8,0},{9,1},... | collective-permute-start | bytes 2359304 | tf_op jit(solution)/shard_map/ppermute | solution.py:686
  118.2 11.9 %collective-permute-start.17 = (bf16[1024,1024]{1,0:T(8,128)(2,1)S(1)}, bf16[1024,1024]{1,0:T(8,128)(2,1)S(1)}, u32[]{:S(2)}, u32[]{:S(2)}) collective-permute-start(bf16[1024,1024]{1,0:T(8,128)(2,1)S(1)} %get-tuple-element.269), channel_id=1, source_target_pairs={{0,1},{1,0},{2,3},{3,2},{4,5},{5,4},{6,7},{7,6},{8,9},{9,8},{10,11... | collective-permute-start | bytes 6291464 | tf_op jit(solution)/shard_map/ppermute | solution.py:686
  118.3 6.7 %collective-permute-start.19 = (bf16[256,128]{1,0:T(8,128)(2,1)S(1)}, bf16[256,128]{1,0:T(8,128)(2,1)S(1)}, u32[]{:S(2)}, u32[]{:S(2)}) collective-permute-start(bf16[256,128]{1,0:T(8,128)(2,1)S(1)} %get-tuple-element.273), channel_id=1, source_target_pairs={{0,16},{1,17},{2,18},{3,19},{4,20},{5,21},{6,22},{7,23},{8,24},{9,... | collective-permute-start | bytes 196616 | tf_op jit(solution)/shard_map/ppermute | solution.py:686
  120.9 4.2 %collective-permute-start.22 = (f32[8,128]{1,0:T(8,128)S(1)}, f32[8,128]{1,0:T(8,128)S(1)}, u32[]{:S(2)}, u32[]{:S(2)}) collective-permute-start(f32[8,128]{1,0:T(8,128)S(1)} %get-tuple-element.268.refs_4_), channel_id=1, source_target_pairs={{0,1},{1,0},{2,3},{3,2},{4,5},{5,4},{6,7},{7,6},{8,9},{9,8},{10,11... | collective-permute-start | bytes 12296 | tf_op jit(solution)/shard_map/ppermute | solution.py:686
  127.0 7.8 %collective-permute-start.25 = (bf16[512,384]{1,0:T(8,128)(2,1)S(1)}, bf16[512,384]{1,0:T(8,128)(2,1)S(1)}, u32[]{:S(2)}, u32[]{:S(2)}) collective-permute-start(bf16[512,384]{1,0:T(8,128)(2,1)S(1)} %get-tuple-element.285), channel_id=1, source_target_pairs={{0,4},{1,3},{2,6},{3,1},{4,0},{5,7},{6,2},{7,5},{8,12},{9,11},{10,... | collective-permute-start | bytes 1179656 | tf_op jit(solution)/shard_map/ppermute | solution.py:686
  129.7 34.0 %collective-permute-start.29 = (bf16[256,2048]{1,0:T(8,128)(2,1)S(1)}, bf16[256,2048]{1,0:T(8,128)(2,1)S(1)}, u32[]{:S(2)}, u32[]{:S(2)}) collective-permute-start(bf16[256,2048]{1,0:T(8,128)(2,1)S(1)} %get-tuple-element.295), channel_id=1, source_target_pairs={{0,8},{1,9},{2,10},{3,11},{4,12},{5,13},{6,14},{7,15},{8,0},{9,1},... | collective-permute-start | bytes 3145736 | tf_op jit(solution)/shard_map/ppermute | solution.py:686
  131.9 6.9 %collective-permute-start.26 = (f32[8,128]{1,0:T(8,128)S(1)}, f32[8,128]{1,0:T(8,128)S(1)}, u32[]{:S(2)}, u32[]{:S(2)}) collective-permute-start(f32[8,128]{1,0:T(8,128)S(1)} %get-tuple-element.282.refs_5_), channel_id=1, source_target_pairs={{0,1},{1,0},{2,3},{3,2},{4,5},{5,4},{6,7},{7,6},{8,9},{9,8},{10,11... | collective-permute-start | bytes 12296 | tf_op jit(solution)/shard_map/ppermute | solution.py:686
  133.2 6.9 %collective-permute-start.24 = (bf16[1024,512]{1,0:T(8,128)(2,1)S(1)}, bf16[1024,512]{1,0:T(8,128)(2,1)S(1)}, u32[]{:S(2)}, u32[]{:S(2)}) collective-permute-start(bf16[1024,512]{1,0:T(8,128)(2,1)S(1)} %get-tuple-element.283), channel_id=1, source_target_pairs={{0,1},{1,0},{2,3},{3,2},{4,5},{5,4},{6,7},{7,6},{8,9},{9,8},{10,11... | collective-permute-start | bytes 3145736 | tf_op jit(solution)/shard_map/ppermute | solution.py:686
  135.1 21.6 %collective-permute-start.30 = (bf16[256,384]{1,0:T(8,128)(2,1)S(1)}, bf16[256,384]{1,0:T(8,128)(2,1)S(1)}, u32[]{:S(2)}, u32[]{:S(2)}) collective-permute-start(bf16[256,384]{1,0:T(8,128)(2,1)S(1)} %get-tuple-element.299), channel_id=1, source_target_pairs={{0,16},{1,17},{2,18},{3,19},{4,20},{5,21},{6,22},{7,23},{8,24},{9,... | collective-permute-start | bytes 589832 | tf_op jit(solution)/shard_map/ppermute | solution.py:686
  137.0 19.8 %collective-permute-start.33 = (bf16[512,1024]{1,0:T(8,128)(2,1)S(1)}, bf16[512,1024]{1,0:T(8,128)(2,1)S(1)}, u32[]{:S(2)}, u32[]{:S(2)}) collective-permute-start(bf16[512,1024]{1,0:T(8,128)(2,1)S(1)} %get-tuple-element.306), channel_id=1, source_target_pairs={{0,2},{1,5},{2,0},{3,7},{4,6},{5,1},{6,4},{7,3},{8,10},{9,13},{10,... | collective-permute-start | bytes 3145736 | tf_op jit(solution)/shard_map/ppermute | solution.py:686
  140.1 13.7 %collective-permute-start.31 = (bf16[1024,512]{1,0:T(8,128)(2,1)S(1)}, bf16[1024,512]{1,0:T(8,128)(2,1)S(1)}, u32[]{:S(2)}, u32[]{:S(2)}) collective-permute-start(bf16[1024,512]{1,0:T(8,128)(2,1)S(1)} %get-tuple-element.300), channel_id=1, source_target_pairs={{0,1},{1,0},{2,3},{3,2},{4,5},{5,4},{6,7},{7,6},{8,9},{9,8},{10,11... | collective-permute-start | bytes 3145736 | tf_op jit(solution)/shard_map/ppermute | solution.py:686
  153.2 11.4 %collective-permute-start.27 = (f32[1,9216]{1,0:T(1,128)S(1)}, f32[1,9216]{1,0:T(1,128)S(1)}, u32[]{:S(2)}, u32[]{:S(2)}) collective-permute-start(f32[1,9216]{1,0:T(1,128)S(1)} %get-tuple-element.291.refs_0_), channel_id=1, source_target_pairs={{0,1},{1,0},{2,3},{3,2},{4,5},{5,4},{6,7},{7,6},{8,9},{9,8},{10,11... | collective-permute-start | bytes 110600 | tf_op jit(solution)/shard_map/ppermute | solution.py:686
  153.8 10.7 %collective-permute-start.28 = (bf16[512,512]{1,0:T(8,128)(2,1)S(1)}, bf16[512,512]{1,0:T(8,128)(2,1)S(1)}, u32[]{:S(2)}, u32[]{:S(2)}) collective-permute-start(bf16[512,512]{1,0:T(8,128)(2,1)S(1)} %get-tuple-element.293), channel_id=1, source_target_pairs={{0,2},{1,5},{2,0},{3,7},{4,6},{5,1},{6,4},{7,3},{8,10},{9,13},{10,... | collective-permute-start | bytes 1572872 | tf_op jit(solution)/shard_map/ppermute | solution.py:686
  156.8 14.6 %collective-permute-start.35 = (bf16[512,512]{1,0:T(8,128)(2,1)S(1)}, bf16[512,512]{1,0:T(8,128)(2,1)S(1)}, u32[]{:S(2)}, u32[]{:S(2)}) collective-permute-start(bf16[512,512]{1,0:T(8,128)(2,1)S(1)} %get-tuple-element.314), channel_id=1, source_target_pairs={{0,2},{1,5},{2,0},{3,7},{4,6},{5,1},{6,4},{7,3},{8,10},{9,13},{10,... | collective-permute-start | bytes 1572872 | tf_op jit(solution)/shard_map/ppermute | solution.py:686
  158.6 27.9 %collective-permute-start.40 = (bf16[256,1024]{1,0:T(8,128)(2,1)S(1)}, bf16[256,1024]{1,0:T(8,128)(2,1)S(1)}, u32[]{:S(2)}, u32[]{:S(2)}) collective-permute-start(bf16[256,1024]{1,0:T(8,128)(2,1)S(1)} %get-tuple-element.327), channel_id=1, source_target_pairs={{0,8},{1,9},{2,10},{3,11},{4,12},{5,13},{6,14},{7,15},{8,0},{9,1},... | collective-permute-start | bytes 1572872 | tf_op jit(solution)/shard_map/ppermute | solution.py:686
  163.9 10.0 %collective-permute-start.38 = (bf16[128,2048]{1,0:T(8,128)(2,1)S(1)}, bf16[128,2048]{1,0:T(8,128)(2,1)S(1)}, u32[]{:S(2)}, u32[]{:S(2)}) collective-permute-start(bf16[128,2048]{1,0:T(8,128)(2,1)S(1)} %get-tuple-element.321), channel_id=1, source_target_pairs={{0,4},{1,3},{2,6},{3,1},{4,0},{5,7},{6,2},{7,5},{8,12},{9,11},{10,... | collective-permute-start | bytes 1572872 | tf_op jit(solution)/shard_map/ppermute | solution.py:686
  164.6 8.4 %collective-permute-start.34 = (f32[1,9216]{1,0:T(1,128)S(1)}, f32[1,9216]{1,0:T(1,128)S(1)}, u32[]{:S(2)}, u32[]{:S(2)}) collective-permute-start(f32[1,9216]{1,0:T(1,128)S(1)} %get-tuple-element.312.refs_0_), channel_id=1, source_target_pairs={{0,2},{1,3},{2,0},{3,1},{4,6},{5,7},{6,4},{7,5},{8,10},{9,11},{10,... | collective-permute-start | bytes 110600 | tf_op jit(solution)/shard_map/ppermute | solution.py:686
  165.5 20.8 %collective-permute-start.37 = (bf16[256,512]{1,0:T(8,128)(2,1)S(1)}, bf16[256,512]{1,0:T(8,128)(2,1)S(1)}, u32[]{:S(2)}, u32[]{:S(2)}) collective-permute-start(bf16[256,512]{1,0:T(8,128)(2,1)S(1)} %get-tuple-element.319), channel_id=1, source_target_pairs={{0,8},{1,9},{2,10},{3,11},{4,12},{5,13},{6,14},{7,15},{8,0},{9,1},... | collective-permute-start | bytes 786440 | tf_op jit(solution)/shard_map/ppermute | solution.py:686
  171.6 21.6 %collective-permute-start.42 = (bf16[256,512]{1,0:T(8,128)(2,1)S(1)}, bf16[256,512]{1,0:T(8,128)(2,1)S(1)}, u32[]{:S(2)}, u32[]{:S(2)}) collective-permute-start(bf16[256,512]{1,0:T(8,128)(2,1)S(1)} %get-tuple-element.332), channel_id=1, source_target_pairs={{0,8},{1,9},{2,10},{3,11},{4,12},{5,13},{6,14},{7,15},{8,0},{9,1},... | collective-permute-start | bytes 786440 | tf_op jit(solution)/shard_map/ppermute | solution.py:686
  173.0 13.4 %collective-permute-start.36 = (f32[1,9216]{1,0:T(1,128)S(1)}, f32[1,9216]{1,0:T(1,128)S(1)}, u32[]{:S(2)}, u32[]{:S(2)}) collective-permute-start(f32[1,9216]{1,0:T(1,128)S(1)} %get-tuple-element.317.refs_0_), channel_id=1, source_target_pairs={{0,4},{1,5},{2,6},{3,7},{4,0},{5,1},{6,2},{7,3},{8,12},{9,13},{10,... | collective-permute-start | bytes 110600 | tf_op jit(solution)/shard_map/ppermute | solution.py:686
  174.0 24.4 %collective-permute-start.49 = (bf16[64,2048]{1,0:T(8,128)(2,1)S(1)}, bf16[64,2048]{1,0:T(8,128)(2,1)S(1)}, u32[]{:S(2)}, u32[]{:S(2)}) collective-permute-start(bf16[64,2048]{1,0:T(8,128)(2,1)S(1)} %get-tuple-element.352), channel_id=1, source_target_pairs={{0,16},{1,17},{2,18},{3,19},{4,20},{5,21},{6,22},{7,23},{8,24},{9,... | collective-permute-start | bytes 786440 | tf_op jit(solution)/shard_map/ppermute | solution.py:686
  186.4 4.9 %collective-permute-start.39 = (f32[1,9216]{1,0:T(1,128)S(1)}, f32[1,9216]{1,0:T(1,128)S(1)}, u32[]{:S(2)}, u32[]{:S(2)}) collective-permute-start(f32[1,9216]{1,0:T(1,128)S(1)} %get-tuple-element.325.refs_0_), channel_id=1, source_target_pairs={{0,8},{1,9},{2,10},{3,11},{4,12},{5,13},{6,14},{7,15},{8,0},{9,1},... | collective-permute-start | bytes 110600 | tf_op jit(solution)/shard_map/ppermute | solution.py:686
  186.7 9.6 %collective-permute-start.43 = (bf16[128,1024]{1,0:T(8,128)(2,1)S(1)}, bf16[128,1024]{1,0:T(8,128)(2,1)S(1)}, u32[]{:S(2)}, u32[]{:S(2)}) collective-permute-start(bf16[128,1024]{1,0:T(8,128)(2,1)S(1)} %get-tuple-element.337), channel_id=1, source_target_pairs={{0,4},{1,3},{2,6},{3,1},{4,0},{5,7},{6,2},{7,5},{8,12},{9,11},{10,... | collective-permute-start | bytes 786440 | tf_op jit(solution)/shard_map/ppermute | solution.py:686
  187.2 9.1 %collective-permute-start.44 = (bf16[128,512]{1,0:T(8,128)(2,1)S(1)}, bf16[128,512]{1,0:T(8,128)(2,1)S(1)}, u32[]{:S(2)}, u32[]{:S(2)}) collective-permute-start(bf16[128,512]{1,0:T(8,128)(2,1)S(1)} %get-tuple-element.339), channel_id=1, source_target_pairs={{0,4},{1,3},{2,6},{3,1},{4,0},{5,7},{6,2},{7,5},{8,12},{9,11},{10,... | collective-permute-start | bytes 393224 | tf_op jit(solution)/shard_map/ppermute | solution.py:686
  191.4 4.9 %collective-permute-start.41 = (f32[1,9216]{1,0:T(1,128)S(1)}, f32[1,9216]{1,0:T(1,128)S(1)}, u32[]{:S(2)}, u32[]{:S(2)}) collective-permute-start(f32[1,9216]{1,0:T(1,128)S(1)} %get-tuple-element.330.refs_0_), channel_id=1, source_target_pairs={{0,16},{1,17},{2,18},{3,19},{4,20},{5,21},{6,22},{7,23},{8,24},{9,... | collective-permute-start | bytes 110600 | tf_op jit(solution)/shard_map/ppermute | solution.py:686
  193.3 5.0 %collective-permute-start.46 = (bf16[128,512]{1,0:T(8,128)(2,1)S(1)}, bf16[128,512]{1,0:T(8,128)(2,1)S(1)}, u32[]{:S(2)}, u32[]{:S(2)}) collective-permute-start(bf16[128,512]{1,0:T(8,128)(2,1)S(1)} %get-tuple-element.345), channel_id=1, source_target_pairs={{0,4},{1,3},{2,6},{3,1},{4,0},{5,7},{6,2},{7,5},{8,12},{9,11},{10,... | collective-permute-start | bytes 393224 | tf_op jit(solution)/shard_map/ppermute | solution.py:686
  198.5 6.5 %collective-permute-start.48 = (bf16[64,512]{1,0:T(8,128)(2,1)S(1)}, bf16[64,512]{1,0:T(8,128)(2,1)S(1)}, u32[]{:S(2)}, u32[]{:S(2)}) collective-permute-start(bf16[64,512]{1,0:T(8,128)(2,1)S(1)} %get-tuple-element.350), channel_id=1, source_target_pairs={{0,16},{1,17},{2,18},{3,19},{4,20},{5,21},{6,22},{7,23},{8,24},{9,... | collective-permute-start | bytes 196616 | tf_op jit(solution)/shard_map/ppermute | solution.py:686
  205.1 3.7 %collective-permute-start.51 = (bf16[32,512]{1,0:T(8,128)(2,1)S(1)}, bf16[32,512]{1,0:T(8,128)(2,1)S(1)}, u32[]{:S(2)}, u32[]{:S(2)}) collective-permute-start(bf16[32,512]{1,0:T(8,128)(2,1)S(1)} %get-tuple-element.359), channel_id=1, source_target_pairs={{0,1},{1,0},{2,3},{3,2},{4,5},{5,4},{6,7},{7,6},{8,9},{9,8},{10,11... | collective-permute-start | bytes 98312 | tf_op jit(solution)/shard_map/ppermute | solution.py:686
  205.8 12.0 %collective-permute-start.45 = (bf16[64,1024]{1,0:T(8,128)(2,1)S(1)}, bf16[64,1024]{1,0:T(8,128)(2,1)S(1)}, u32[]{:S(2)}, u32[]{:S(2)}) collective-permute-start(bf16[64,1024]{1,0:T(8,128)(2,1)S(1)} %get-tuple-element.343), channel_id=1, source_target_pairs={{0,16},{1,17},{2,18},{3,19},{4,20},{5,21},{6,22},{7,23},{8,24},{9,... | collective-permute-start | bytes 393224 | tf_op jit(solution)/shard_map/ppermute | solution.py:686
  205.8 12.0 %collective-permute-start.47 = (bf16[64,512]{1,0:T(8,128)(2,1)S(1)}, bf16[64,512]{1,0:T(8,128)(2,1)S(1)}, u32[]{:S(2)}, u32[]{:S(2)}) collective-permute-start(bf16[64,512]{1,0:T(8,128)(2,1)S(1)} %get-tuple-element.348), channel_id=1, source_target_pairs={{0,16},{1,17},{2,18},{3,19},{4,20},{5,21},{6,22},{7,23},{8,24},{9,... | collective-permute-start | bytes 196616 | tf_op jit(solution)/shard_map/ppermute | solution.py:686
  (27 other events, 123.1 us)
where the time goes:
time: 225 us; the launch traced here: 221 us
  Pallas kernels  121 us (54%)
  starting transfers between devices  48.3 us (21%)
  waiting for transfers between devices  44 us (20%)
  local copies, waits for them, and re-layouts  4.52 us (2%)
    pallas_call x62, Pallas kernels, kernel_call(): pl.pallas_call(wrapped, name=body.__qualname__.split('.')[0], in_specs=[S...  121 us
    ppermute x54, starting transfers between devices, swap(): return lax.ppermute(v, AXES, pairs)  48.3 us
    ppermute x54, waiting for transfers between devices, swap(): return lax.ppermute(v, AXES, pairs)  44 us
  transfers between devices with their start and end apart: 54, of which 13 were waited for; matrix products, arithmetic and copies ran while one was open for 1% of the time, Pallas kernels for 44%

commit v1 on v0

--- a/solution.py
+++ b/solution.py
@@ -13,10 +13,10 @@
 AXES = ("rows", "seq")
 DOWN = (1, 3)
 STEPS = (
-    "turn", "d1o", "d2o", "d1m", "dn2", "d2m", "n2t", "uo", "d1f", "mixer", "d1f", "merge", "um", "layer", "d2f",
-    "d1f", "back", "att", "q1o", "d1f", "d2f", "d1a", "uf", "q1m", "po", "d2f", "q2o", "pm", "dn1", "q2m", "d2f",
-    "q1f", "de", "small", "uf", "pf", "small", "q2f", "small", "uf", "pf", "small", "q1f", "small", "q2f", "small",
-    "pf", "q1f", "q2f", "uf", "ue", "pf", "pe", "q2f", "q1f", "qe",
+    "turn", "d1o", "d2o", "d1m", "dn2", "d2m", "n2t", "uo", "d1f", "mixer", "d1f", "merge", "um", "d2f",
+    "layer", "d1f", "back", "q1o", "att", "d1f", "d2f", "d1a", "uf", "q1m", "q2o", "po", "d2f", "q2m",
+    "pm", "dn1", "d2f", "q1f", "de", "small", "uf", "pf", "small", "q2f", "small", "uf", "pf", "small",
+    "q1f", "small", "q2f", "small", "pf", "q1f", "q2f", "uf", "ue", "pf", "pe", "q2f", "q1f", "qe",
 )
 SUMS = 64
 DEPTH = 80

time: 225 us -> 225 us (level)
  waiting for transfers between devices: 44 us -> 46.6 us
    ppermute x54 -> x55, waiting for transfers between devices: 44 us -> 46.6 us  [swap(): return lax.ppermute(v, AXES, pairs)]
    pallas_call x62, Pallas kernels: 121 us -> 119 us  [kernel_call(): pl.pallas_call(wrapped, name=body.__qualname__.split('.')[0], in_specs=[S...]
    ppermute x54 -> x55, starting transfers between devices: 48.3 us -> 46.6 us  [swap(): return lax.ppermute(v, AXES, pairs)]
  transfers between devices with their start and end apart: 54 -> 55, of which waited for: 13 -> 15; matrix products, arithmetic and copies ran while one was open for 1% -> 1% of each run, Pallas kernels for 44% -> 43%
where the time goes in v1:
time: 225 us; the launch traced here: 220 us
  Pallas kernels  119 us (53%)
  starting transfers between devices  46.6 us (21%)
  waiting for transfers between devices  46.6 us (21%)
  local copies, waits for them, and re-layouts  5.1 us (2%)
    pallas_call x62, Pallas kernels, kernel_call(): pl.pallas_call(wrapped, name=body.__qualname__.split('.')[0], in_specs=[S...  119 us
    ppermute x55, starting transfers between devices, swap(): return lax.ppermute(v, AXES, pairs)  46.6 us
    ppermute x55, waiting for transfers between devices, swap(): return lax.ppermute(v, AXES, pairs)  46.6 us
  transfers between devices with their start and end apart: 55, of which 15 were waited for; matrix products, arithmetic and copies ran while one was open for 1% of the time, Pallas kernels for 43%

profile of v1, /device:TPU:0, one launch (start us, length us, event | category | flops | bytes accessed | tf_op | source)
XLA Modules:
  0.0 220.1 jit_solution(196320565173505719)
XLA Ops:
  1.3 6.5 %keys_values.1 = (bf16[512,1024]{1,0:T(8,128)(2,1)S(1)}, bf16[512,1024]{1,0:T(8,128)(2,1)S(1)}, bf16[512,1024]{1,0:T(8,128)(2,1)S(1)}, bf16[2,8,80,128]{3,2,1,0:...) custom-call(s32[2,4]{1,0:T(2,128)S(1)} %broadcast_subtract_fusion.re, ...), custom_call_target="tpu_custom_call" | custom-call | flops 73000001536 | bytes 1 | tf_op jit(solution)/shard_map/keys_values/pallas_call | solution.py:79
  9.8 3.7 %queries.1 = (bf16[512,1024]{1,0:T(8,128)(2,1)S(1)}, bf16[1024,512]{1,0:T(8,128)(2,1)S(1)}, f32[8,128]{1,0:T(8,128)S(1)}) custom-call(s32[4,32]{1,0:T(4,128)S(1)} %add_add_fusion.refs_0_, bf16[512,1024]{1,0:T(8,128)(2,1)S(1)} %get-tuple-element.193.refs_1_, bf16[1024,3072]{1,0:T(8,128)(2,1)} %refs_8_.3, ...), custom_call_target="tpu_custom_call" | custom-call | flops 38999998464 | bytes 1 | tf_op jit(solution)/shard_map/queries/pallas_call | solution.py:79
  14.3 4.8 %collective-permute-start.1 = (bf16[2,8,80,128]{3,2,1,0:T(8,128)(2,1)S(1)}, bf16[2,8,80,128]{3,2,1,0:T(8,128)(2,1)S(1)}, u32[]{:S(2)}, u32[]{:S(2)}) collective-permute-start(bf16[2,8,80,128]{3,2,1,0:T(8,128)(2,1)S(1)} %get-tuple-element.201), channel_id=1, source_target_pairs={{0,2},{1,3},{4,6},{5,7},{8,10},{9,11},{12,14},{13,15},{16,18},{17,... | collective-permute-start | bytes 983048 | tf_op jit(solution)/shard_map/ppermute | solution.py:686
  19.1 4.8 %attend_inside.1 = (f32[512,1024]{1,0:T(8,128)S(1)}, f32[512,1024]{1,0:T(8,128)S(1)}, bf16[4096,1024]{1,0:T(8,128)(2,1)S(1)}, bf16[1024,1024]{1,0:T(8,128)(2,1)S...) custom-call(s32[2,4]{1,0:T(2,128)S(1)} %broadcast_subtract_fusion.refs_0_, ...), custom_call_target="tpu_custom_call" | custom-call | flops 57000001536 | bytes 1 | tf_op jit(solution)/shard_map/attend_inside/pallas_call | solution.py:79
  23.9 4.6 %active_grads.1 = (bf16[512,4096]{1,0:T(8,128)(2,1)S(1)}, f32[8,128]{1,0:T(8,128)S(1)}) custom-call(bf16[512,1024]{1,0:T(8,128)(2,1)S(1)} %get-tuple-element.209.refs_0_.refs_14_.refs_8_.refs_2_.refs_3_, bf16[4096,1024]{1,0:T(8,128)(2,1)S(1)} %get-tuple-element.210.refs_1_, ...), custom_call_target="tpu_custom_call" | custom-call | flops 44999999488 | bytes 1 | tf_op jit(solution)/shard_map/active_grads/pallas_call | solution.py:79
  28.5 4.4 %attend_join.1 = (bf16[512,1024]{1,0:T(8,128)(2,1)S(1)}, f32[512,1024]{1,0:T(8,128)S(1)}, f32[512,1024]{1,0:T(8,128)S(1)}, bf16[512,1024]{1,0:T(8,128)(2,1)S(1)}...) custom-call(s32[2,4]{1,0:T(2,128)S(1)} %broadcast_subtract_fusion.refs_0_, f32[2,2]{1,0:T(2,128)S(1)} %pad_maximum_fusion.refs_1_, ...), custom_call_target="tpu_custom_call" | custom-call | flops 49999998976 | bytes 1 | tf_op jit(solution)/shard_map/attend_join/pallas_call | solution.py:79
  33.0 10.6 %expand.1 = (bf16[512,4096]{1,0:T(8,128)(2,1)S(1)}, bf16[512,4096]{1,0:T(8,128)(2,1)S(1)}, f32[1,4096]{1,0:T(1,128)S(1)}, f32[8,128]{1,0:T(8,128)S(1)}) custom-call(bf16[512,1024]{1,0:T(8,128)(2,1)S(1)} %get-tuple-element.214.refs_0_.refs_4_.refs_5_.refs_6_.refs_1_, bf16[1024,4096]{1,0:T(8,128)(2,1)S(1)} %get-tuple-element.215.refs_1_.refs_3_.refs_4_.refs_5_, ...), custom_call_target="tpu_custom_call" | custom-call | flops 109999996928 | bytes 1 | tf_op jit(solution)/shard_map/expand/pallas_call | solution.py:79
  45.7 1.8 down_grad.4
  47.7 2.9 %down_grad.5 = (bf16[4096,384]{1,0:T(8,128)(2,1)S(1)}, f32[8,128]{1,0:T(8,128)S(1)}) custom-call(s32[4,32]{1,0:T(4,128)S(1)} %copy-done.1, bf16[4096,512]{1,0:T(8,128)(2,1)S(1)} %get-tuple-element.221.refs_1_.refs_6_, bf16[512,1024]{1,0:T(8,128)(2,1)S(1)} %get-tuple-element.209.refs_0_.refs_14_.refs_8_.refs_2_.refs_3_, ...), custom_call_target="tpu_custom_call" | custom-call | flops 34909089792 | bytes 1 | tf_op jit(solution)/shard_map/down_grad/pallas_call | solution.py:79
  51.3 2.3 %down_grad.6 = (bf16[2048,128]{1,0:T(8,128)(2,1)}, bf16[2048,128]{1,0:T(8,128)(2,1)S(1)}, f32[8,128]{1,0:T(8,128)S(1)}) custom-call(s32[4,32]{1,0:T(4,128)S(1)} %copy-done.1, bf16[4096,512]{1,0:T(8,128)(2,1)S(1)} %get-tuple-element.221.refs_1_.refs_6_, bf16[512,1024]{1,0:T(8,128)(2,1)S(1)} %get-tuple-element.209.refs_0_.refs_14_.refs_8_.refs_2_.refs_3_, ...), custom_call_target="tpu_custom_call" | custom-call | flops 11636363264 | bytes 1 | tf_op jit(solution)/shard_map/down_grad/pallas_call | solution.py:79
  53.7 6.7 %second_norm_grads.1 = (f32[512,1024]{1,0:T(8,128)S(1)}, bf16[512,1024]{1,0:T(8,128)(2,1)S(1)}, f32[1,1024]{1,0:T(1,128)S(1)}, f32[1,1024]{1,0:T(1,128)S(1)}, f3...) custom-call(bf16[512,4096]{1,0:T(8,128)(2,1)S(1)} %get-tuple-element.219.refs_1_.refs_3_.refs_4_.refs_0_.re, ...), custom_call_target="tpu_custom_call" | custom-call | flops 70000001024 | bytes 1 | tf_op jit(solution)/shard_map/second_norm_grads/pallas_call | solution.py:79
  60.5 3.0 %down_grad.7 = (bf16[2048,384]{1,0:T(8,128)(2,1)S(1)}, bf16[2048,384]{1,0:T(8,128)(2,1)S(1)}, f32[8,128]{1,0:T(8,128)S(1)}) custom-call(s32[4,32]{1,0:T(4,128)S(1)} %copy-done.1, bf16[4096,512]{1,0:T(8,128)(2,1)S(1)} %get-tuple-element.221.refs_1_.refs_6_, bf16[512,1024]{1,0:T(8,128)(2,1)S(1)} %get-tuple-element.209.refs_0_.refs_14_.refs_8_.refs_2_.refs_3_, ...), custom_call_target="tpu_custom_call" | custom-call | flops 34909089792 | bytes 1 | tf_op jit(solution)/shard_map/down_grad/pallas_call | solution.py:79
  64.3 1.5 collective-permute-start.9
  66.3 2.9 %weight_grad.8 = (bf16[1024,2048]{1,0:T(8,128)(2,1)S(1)}, f32[8,128]{1,0:T(8,128)S(1)}) custom-call(s32[4,32]{1,0:T(4,128)S(1)} %copy-done.1, bf16[1024,512]{1,0:T(8,128)(2,1)S(1)} %get-tuple-element.233.refs_1_, bf16[512,4096]{1,0:T(8,128)(2,1)S(1)} %get-tuple-element.219.refs_1_.refs_3_.refs_4_.refs_0_.refs_2_.refs_6_, ...), custom_call_target="tpu_custom_call" | custom-call | flops 35999997952 | bytes 1 | tf_op jit(solution)/shard_map/weight_grad/pallas_call | solution.py:79
  70.6 1.6 collective-permute-start.11
  72.4 4.3 %mixer_grads.1 = (bf16[512,1024]{1,0:T(8,128)(2,1)S(1)}, f32[512,1024]{1,0:T(8,128)S(1)}, bf16[2,8,80,128]{3,2,1,0:T(8,128)(2,1)S(1)}, f32[8,128]{1,0:T(8,128)S(1)}) custom-call(s32[2,4]{1,0:T(2,128)S(1)} %broadcast_subtract_fusion.refs_0_, bf16[512,1024]{1,0:T(8,128)(2,1)S(1)} %get-tuple-element.236.refs_1_.refs_2_, ...), custom_call_target="tpu_custom_call" | custom-call | flops 49999998976 | bytes 1 | tf_op jit(solution)/shard_map/mixer_grads/pallas_call | solution.py:79
  77.1 2.2 %collective-permute-done.11.refs_1_ = bf16[1024,128]{1,0:T(8,128)(2,1)S(1)} collective-permute-done((bf16[1024,128]{1,0:T(8,128)(2,1)S(1)}, bf16[1024,128]{1,0:T(8,128)(2,1)S(1)}, u32[]{:S(2)}, u32[]{:S(2)}) %collective-permute-start.11) | collective-permute-done | bytes 262176 | tf_op jit(solution)/shard_map/ppermute | solution.py:686
  79.4 1.6 collective-permute-start.15
  83.1 4.2 %weight_grad.9 = (bf16[512,2048]{1,0:T(8,128)(2,1)}, bf16[512,2048]{1,0:T(8,128)(2,1)S(1)}, f32[8,128]{1,0:T(8,128)S(1)}) custom-call(s32[4,32]{1,0:T(4,128)S(1)} %copy-done.1, bf16[1024,512]{1,0:T(8,128)(2,1)S(1)} %get-tuple-element.233.refs_1_, bf16[512,4096]{1,0:T(8,128)(2,1)S(1)} %get-tuple-element.219.refs_1_.refs_3_.refs_4_.refs_0_.refs_2_.refs_6_, ...), custom_call_target="tpu_custom_call" | custom-call | flops 35999997952 | bytes 1 | tf_op jit(solution)/shard_map/weight_grad/pallas_call | solution.py:79
  88.5 1.5 fold.26
  91.6 7.6 %layer_result.1 = (bf16[512,1024]{1,0:T(8,128)(2,1)}, f32[8,128]{1,0:T(8,128)S(1)}) custom-call(bf16[512,4096]{1,0:T(8,128)(2,1)S(1)} %copy-done.10, f32[512,1024]{1,0:T(8,128)S(1)} %copy-done.12, f32[1,1024]{1,0:T(1,128)S(1)} %get-tuple-element.198.refs_7_.refs_8_.refs_6_.refs_13_.refs_4_.refs_2_, bf16[4096,1024]{1,0:T(8,128)(2,1)} %refs_3_.1, ...), custom_call_target="tpu_custom_call" | custom-call | flops 54999998464 | bytes 1 | tf_op jit(solution)/shard_map/layer_result/pallas_call | solution.py:79
  99.3 1.7 collective-permute-start.18
  101.0 2.7 %collective-permute-start.19 = (bf16[256,128]{1,0:T(8,128)(2,1)S(1)}, bf16[256,128]{1,0:T(8,128)(2,1)S(1)}, u32[]{:S(2)}, u32[]{:S(2)}) collective-permute-start(bf16[256,128]{1,0:T(8,128)(2,1)S(1)} %get-tuple-element.273), channel_id=1, source_target_pairs={{0,16},{1,17},{2,18},{3,19},{4,20},{5,21},{6,22},{7,23},{8,24},{9,... | collective-permute-start | bytes 196616 | tf_op jit(solution)/shard_map/ppermute | solution.py:686
  103.7 1.6 collective-permute-start.21
  105.3 10.3 %attend_back.1 = (bf16[512,3072]{1,0:T(8,128)(2,1)S(1)}, f32[8,128]{1,0:T(8,128)S(1)}) custom-call(s32[2,4]{1,0:T(2,128)S(1)} %broadcast_subtract_fusion.refs_0_, f32[2,2]{1,0:T(2,128)S(1)} %pad_maximum_fusion.refs_1_, f32[2,2]{1,0:T(2,128)S(1)} %pad_maximum_fusion.3.refs_2_, bf16[2,8,80,128]{3,2,1,0:T(8,128)(2,1)S(1)} %collective-permute-done.refs_2_.refs_3_, ...), custom_call_target="tpu_custom_call" | custom-call | flops 120000004096 | bytes 1 | tf_op jit(solution)/shard_map/attend_back/pallas_call | solution.py:79
  115.6 1.8 weight_grad.10
  119.1 2.6 %collective-permute-done.22.refs_3_ = f32[8,128]{1,0:T(8,128)S(1)} collective-permute-done((f32[8,128]{1,0:T(8,128)S(1)}, f32[8,128]{1,0:T(8,128)S(1)}, u32[]{:S(2)}, u32[]{:S(2)}) %collective-permute-start.22) | collective-permute-done | bytes 4128 | tf_op jit(solution)/shard_map/ppermute | solution.py:686
  124.4 1.4 collective-permute-start.26
  125.7 2.0 fold.30
  127.8 1.6 collective-permute-start.31
  129.4 1.8 weight_grad.11
  134.5 1.6 collective-permute-start.34
  136.6 2.7 %collective-permute-start.32 = (bf16[256,384]{1,0:T(8,128)(2,1)S(1)}, bf16[256,384]{1,0:T(8,128)(2,1)S(1)}, u32[]{:S(2)}, u32[]{:S(2)}) collective-permute-start(bf16[256,384]{1,0:T(8,128)(2,1)S(1)} %get-tuple-element.301), channel_id=1, source_target_pairs={{0,16},{1,17},{2,18},{3,19},{4,20},{5,21},{6,22},{7,23},{8,24},{9,... | collective-permute-start | bytes 589832 | tf_op jit(solution)/shard_map/ppermute | solution.py:686
  142.5 11.7 %first_norm_grads.1 = (f32[512,1024]{1,0:T(8,128)}, f32[1,9216]{1,0:T(1,128)S(1)}, f32[8,128]{1,0:T(8,128)S(1)}) custom-call(bf16[512,3072]{1,0:T(8,128)(2,1)S(1)} %get-tuple-element.259.refs_2_.refs_3_.refs_4_.refs_0_, bf16[512,1024]{1,0:T(8,128)(2,1)S(1)} %bitcast.33, f32[512,1024]{1,0:T(8,128)S(1)} %copy-done.16, ...), custom_call_target="tpu_custom_call" | custom-call | flops 65000001536 | bytes 1 | tf_op jit(solution)/shard_map/first_norm_grads/pallas_call | solution.py:79
  156.1 1.4 collective-permute-start.36
  157.7 3.6 %collective-permute-start.41 = (bf16[256,1024]{1,0:T(8,128)(2,1)S(1)}, bf16[256,1024]{1,0:T(8,128)(2,1)S(1)}, u32[]{:S(2)}, u32[]{:S(2)}) collective-permute-start(bf16[256,1024]{1,0:T(8,128)(2,1)S(1)} %get-tuple-element.327), channel_id=1, source_target_pairs={{0,8},{1,9},{2,10},{3,11},{4,12},{5,13},{6,14},{7,15},{8,0},{9,1},... | collective-permute-start | bytes 1572872 | tf_op jit(solution)/shard_map/ppermute | solution.py:686
  161.3 1.4 place.4
  164.9 8.9 %collective-permute-done.36.refs_1_ = bf16[512,512]{1,0:T(8,128)(2,1)S(1)} collective-permute-done((bf16[512,512]{1,0:T(8,128)(2,1)S(1)}, bf16[512,512]{1,0:T(8,128)(2,1)S(1)}, u32[]{:S(2)}, u32[]{:S(2)}) %collective-permute-start.36) | collective-permute-done | bytes 524320 | tf_op jit(solution)/shard_map/ppermute | solution.py:686
  175.1 10.2 %collective-permute-done.38.refs_1_ = bf16[256,512]{1,0:T(8,128)(2,1)S(1)} collective-permute-done((bf16[256,512]{1,0:T(8,128)(2,1)S(1)}, bf16[256,512]{1,0:T(8,128)(2,1)S(1)}, u32[]{:S(2)}, u32[]{:S(2)}) %collective-permute-start.38) | collective-permute-done | bytes 262176 | tf_op jit(solution)/shard_map/ppermute | solution.py:686
  185.7 2.0 collective-permute-start.45
  187.8 2.8 %collective-permute-done.40.refs_1_ = f32[1,9216]{1,0:T(1,128)S(1)} collective-permute-done((f32[1,9216]{1,0:T(1,128)S(1)}, f32[1,9216]{1,0:T(1,128)S(1)}, u32[]{:S(2)}, u32[]{:S(2)}) %collective-permute-start.40) | collective-permute-done | bytes 36896 | tf_op jit(solution)/shard_map/ppermute | solution.py:686
  190.6 2.4 %collective-permute-start.42 = (f32[1,9216]{1,0:T(1,128)S(1)}, f32[1,9216]{1,0:T(1,128)S(1)}, u32[]{:S(2)}, u32[]{:S(2)}) collective-permute-start(f32[1,9216]{1,0:T(1,128)S(1)} %get-tuple-element.330.refs_0_), channel_id=1, source_target_pairs={{0,16},{1,17},{2,18},{3,19},{4,20},{5,21},{6,22},{7,23},{8,24},{9,... | collective-permute-start | bytes 110600 | tf_op jit(solution)/shard_map/ppermute | solution.py:686
  194.0 1.5 collective-permute-done.42.refs_1_
  195.5 2.5 %collective-permute-done.47.refs_1_ = bf16[128,512]{1,0:T(8,128)(2,1)S(1)} collective-permute-done((bf16[128,512]{1,0:T(8,128)(2,1)S(1)}, bf16[128,512]{1,0:T(8,128)(2,1)S(1)}, u32[]{:S(2)}, u32[]{:S(2)}) %collective-permute-start.47) | collective-permute-done | bytes 131104 | tf_op jit(solution)/shard_map/ppermute | solution.py:686
  199.6 1.4 place.5
  201.0 3.8 %collective-permute-done.49.refs_1_ = bf16[64,512]{1,0:T(8,128)(2,1)S(1)} collective-permute-done((bf16[64,512]{1,0:T(8,128)(2,1)S(1)}, bf16[64,512]{1,0:T(8,128)(2,1)S(1)}, u32[]{:S(2)}, u32[]{:S(2)}) %collective-permute-start.49) | collective-permute-done | bytes 65568 | tf_op jit(solution)/shard_map/ppermute | solution.py:686
  205.5 2.9 %collective-permute-start.48 = (bf16[64,512]{1,0:T(8,128)(2,1)S(1)}, bf16[64,512]{1,0:T(8,128)(2,1)S(1)}, u32[]{:S(2)}, u32[]{:S(2)}) collective-permute-start(bf16[64,512]{1,0:T(8,128)(2,1)S(1)} %get-tuple-element.348), channel_id=1, source_target_pairs={{0,16},{1,17},{2,18},{3,19},{4,20},{5,21},{6,22},{7,23},{8,24},{9,... | collective-permute-start | bytes 196616 | tf_op jit(solution)/shard_map/ppermute | solution.py:686
  209.7 7.3 %collective-permute-done.48.refs_1_ = bf16[64,512]{1,0:T(8,128)(2,1)S(1)} collective-permute-done((bf16[64,512]{1,0:T(8,128)(2,1)S(1)}, bf16[64,512]{1,0:T(8,128)(2,1)S(1)}, u32[]{:S(2)}, u32[]{:S(2)}) %collective-permute-start.48) | collective-permute-done | bytes 65568 | tf_op jit(solution)/shard_map/ppermute | solution.py:686
  (184 shorter events, 39.2 us)
Async XLA Ops:
  8.8 4.8 %collective-permute-start = (bf16[2,8,80,128]{3,2,1,0:T(8,128)(2,1)S(1)}, bf16[2,8,80,128]{3,2,1,0:T(8,128)(2,1)S(1)}, u32[]{:S(2)}, u32[]{:S(2)}) collective-permute-start(bf16[2,8,80,128]{3,2,1,0:T(8,128)(2,1)S(1)} %get-tuple-element.192.refs_1_), channel_id=1, source_target_pairs={{0,1},{1,0},{2,3},{3,2},{4,5},{5,4},{6,7},{7,6},{8,9},{9,8},{10,11... | collective-permute-start | bytes 983048 | tf_op jit(solution)/shard_map/ppermute | solution.py:686
  14.3 14.2 %collective-permute-start.1 = (bf16[2,8,80,128]{3,2,1,0:T(8,128)(2,1)S(1)}, bf16[2,8,80,128]{3,2,1,0:T(8,128)(2,1)S(1)}, u32[]{:S(2)}, u32[]{:S(2)}) collective-permute-start(bf16[2,8,80,128]{3,2,1,0:T(8,128)(2,1)S(1)} %get-tuple-element.201), channel_id=1, source_target_pairs={{0,2},{1,3},{4,6},{5,7},{8,10},{9,11},{12,14},{13,15},{16,18},{17,... | collective-permute-start | bytes 983048 | tf_op jit(solution)/shard_map/ppermute | solution.py:686
  43.6 4.1 %collective-permute-start.2 = (f32[8,128]{1,0:T(8,128)S(1)}, f32[8,128]{1,0:T(8,128)S(1)}, u32[]{:S(2)}, u32[]{:S(2)}) collective-permute-start(f32[8,128]{1,0:T(8,128)S(1)} %get-tuple-element.220.refs_8_), channel_id=1, source_target_pairs={{0,1},{1,0},{2,3},{3,2},{4,5},{5,4},{6,7},{7,6},{8,9},{9,8},{10,11... | collective-permute-start | bytes 12296 | tf_op jit(solution)/shard_map/ppermute | solution.py:686
  47.5 3.7 %collective-permute-start.4 = (bf16[4096,128]{1,0:T(8,128)(2,1)S(1)}, bf16[4096,128]{1,0:T(8,128)(2,1)S(1)}, u32[]{:S(2)}, u32[]{:S(2)}) collective-permute-start(bf16[4096,128]{1,0:T(8,128)(2,1)S(1)} %get-tuple-element.225), channel_id=1, source_target_pairs={{0,1},{1,0},{2,3},{3,2},{4,5},{5,4},{6,7},{7,6},{8,9},{9,8},{10,11... | collective-permute-start | bytes 3145736 | tf_op jit(solution)/shard_map/ppermute | solution.py:686
  50.7 9.8 %collective-permute-start.3 = (bf16[4096,384]{1,0:T(8,128)(2,1)S(1)}, bf16[4096,384]{1,0:T(8,128)(2,1)S(1)}, u32[]{:S(2)}, u32[]{:S(2)}) collective-permute-start(bf16[4096,384]{1,0:T(8,128)(2,1)S(1)} %get-tuple-element.224), channel_id=1, source_target_pairs={{0,1},{1,0},{2,3},{3,2},{4,5},{5,4},{6,7},{7,6},{8,9},{9,8},{10,11... | collective-permute-start | bytes 9437192 | tf_op jit(solution)/shard_map/ppermute | solution.py:686
  51.1 9.3 %collective-permute-start.5 = (f32[8,128]{1,0:T(8,128)S(1)}, f32[8,128]{1,0:T(8,128)S(1)}, u32[]{:S(2)}, u32[]{:S(2)}) collective-permute-start(f32[8,128]{1,0:T(8,128)S(1)} %get-tuple-element.226.refs_10_), channel_id=1, source_target_pairs={{0,1},{1,0},{2,3},{3,2},{4,5},{5,4},{6,7},{7,6},{8,9},{9,8},{10,11... | collective-permute-start | bytes 12296 | tf_op jit(solution)/shard_map/ppermute | solution.py:686
  53.5 15.8 %collective-permute-start.8 = (bf16[2048,128]{1,0:T(8,128)(2,1)}, bf16[2048,128]{1,0:T(8,128)(2,1)}, u32[]{:S(2)}, u32[]{:S(2)}) collective-permute-start(bf16[2048,128]{1,0:T(8,128)(2,1)} %get-tuple-element.240), channel_id=1, source_target_pairs={{0,2},{1,5},{2,0},{3,7},{4,6},{5,1},{6,4},{7,3},{8,10},{9,13},{10,... | collective-permute-start | bytes 1572872 | tf_op jit(solution)/shard_map/ppermute | solution.py:686
  64.3 5.0 %collective-permute-start.9 = (f32[8,128]{1,0:T(8,128)S(1)}, f32[8,128]{1,0:T(8,128)S(1)}, u32[]{:S(2)}, u32[]{:S(2)}) collective-permute-start(f32[8,128]{1,0:T(8,128)S(1)} %get-tuple-element.232.refs_2_), channel_id=1, source_target_pairs={{0,1},{1,0},{2,3},{3,2},{4,5},{5,4},{6,7},{7,6},{8,9},{9,8},{10,11... | collective-permute-start | bytes 12296 | tf_op jit(solution)/shard_map/ppermute | solution.py:686
  65.8 22.6 %collective-permute-start.6 = (bf16[2048,384]{1,0:T(8,128)(2,1)S(1)}, bf16[2048,384]{1,0:T(8,128)(2,1)S(1)}, u32[]{:S(2)}, u32[]{:S(2)}) collective-permute-start(bf16[2048,384]{1,0:T(8,128)(2,1)S(1)} %get-tuple-element.231), channel_id=1, source_target_pairs={{0,2},{1,5},{2,0},{3,7},{4,6},{5,1},{6,4},{7,3},{8,10},{9,13},{10,... | collective-permute-start | bytes 4718600 | tf_op jit(solution)/shard_map/ppermute | solution.py:686
  69.2 13.8 %collective-permute-start.7 = (bf16[1024,2048]{1,0:T(8,128)(2,1)S(1)}, bf16[1024,2048]{1,0:T(8,128)(2,1)S(1)}, u32[]{:S(2)}, u32[]{:S(2)}) collective-permute-start(bf16[1024,2048]{1,0:T(8,128)(2,1)S(1)} %get-tuple-element.235), channel_id=1, source_target_pairs={{0,1},{1,0},{2,3},{3,2},{4,5},{5,4},{6,7},{7,6},{8,9},{9,8},{10,11... | collective-permute-start | bytes 12582920 | tf_op jit(solution)/shard_map/ppermute | solution.py:686
  70.6 8.8 %collective-permute-start.11 = (bf16[1024,128]{1,0:T(8,128)(2,1)S(1)}, bf16[1024,128]{1,0:T(8,128)(2,1)S(1)}, u32[]{:S(2)}, u32[]{:S(2)}) collective-permute-start(bf16[1024,128]{1,0:T(8,128)(2,1)S(1)} %get-tuple-element.245), channel_id=1, source_target_pairs={{0,8},{1,9},{2,10},{3,11},{4,12},{5,13},{6,14},{7,15},{8,0},{9,1},... | collective-permute-start | bytes 786440 | tf_op jit(solution)/shard_map/ppermute | solution.py:686
  72.2 8.8 %collective-permute-start.12 = (f32[8,128]{1,0:T(8,128)S(1)}, f32[8,128]{1,0:T(8,128)S(1)}, u32[]{:S(2)}, u32[]{:S(2)}) collective-permute-start(f32[8,128]{1,0:T(8,128)S(1)} %get-tuple-element.242.refs_9_), channel_id=1, source_target_pairs={{0,1},{1,0},{2,3},{3,2},{4,5},{5,4},{6,7},{7,6},{8,9},{9,8},{10,11... | collective-permute-start | bytes 12296 | tf_op jit(solution)/shard_map/ppermute | solution.py:686
  76.7 4.3 %collective-permute-start.10 = (bf16[2,8,80,128]{3,2,1,0:T(8,128)(2,1)S(1)}, bf16[2,8,80,128]{3,2,1,0:T(8,128)(2,1)S(1)}, u32[]{:S(2)}, u32[]{:S(2)}) collective-permute-start(bf16[2,8,80,128]{3,2,1,0:T(8,128)(2,1)S(1)} %get-tuple-element.243.refs_1_), channel_id=1, source_target_pairs={{0,1},{1,0},{2,3},{3,2},{4,5},{5,4},{6,7},{7,6},{8,9},{9,8},{10,11... | collective-permute-start | bytes 983048 | tf_op jit(solution)/shard_map/ppermute | solution.py:686
  79.4 21.5 %collective-permute-start.15 = (bf16[512,128]{1,0:T(8,128)(2,1)S(1)}, bf16[512,128]{1,0:T(8,128)(2,1)S(1)}, u32[]{:S(2)}, u32[]{:S(2)}) collective-permute-start(bf16[512,128]{1,0:T(8,128)(2,1)S(1)} %get-tuple-element.256), channel_id=1, source_target_pairs={{0,4},{1,3},{2,6},{3,1},{4,0},{5,7},{6,2},{7,5},{8,12},{9,11},{10,... | collective-permute-start | bytes 393224 | tf_op jit(solution)/shard_map/ppermute | solution.py:686
  81.7 8.3 %collective-permute-start.13 = (f32[8,128]{1,0:T(8,128)S(1)}, f32[8,128]{1,0:T(8,128)S(1)}, u32[]{:S(2)}, u32[]{:S(2)}) collective-permute-start(f32[8,128]{1,0:T(8,128)S(1)} %get-tuple-element.248.refs_6_), channel_id=1, source_target_pairs={{0,1},{1,0},{2,3},{3,2},{4,5},{5,4},{6,7},{7,6},{8,9},{9,8},{10,11... | collective-permute-start | bytes 12296 | tf_op jit(solution)/shard_map/ppermute | solution.py:686
  81.8 23.5 %collective-permute-start.14 = (bf16[2,8,80,128]{3,2,1,0:T(8,128)(2,1)S(1)}, bf16[2,8,80,128]{3,2,1,0:T(8,128)(2,1)S(1)}, u32[]{:S(2)}, u32[]{:S(2)}) collective-permute-start(bf16[2,8,80,128]{3,2,1,0:T(8,128)(2,1)S(1)} %get-tuple-element.252), channel_id=1, source_target_pairs={{2,0},{3,1},{6,4},{7,5},{10,8},{11,9},{14,12},{15,13},{18,16},{19,... | collective-permute-start | bytes 983048 | tf_op jit(solution)/shard_map/ppermute | solution.py:686
  99.2 16.4 %collective-permute-start.16 = (f32[8,128]{1,0:T(8,128)S(1)}, f32[8,128]{1,0:T(8,128)S(1)}, u32[]{:S(2)}, u32[]{:S(2)}) collective-permute-start(f32[8,128]{1,0:T(8,128)S(1)} %get-tuple-element.257.refs_2_), channel_id=1, source_target_pairs={{0,1},{1,0},{2,3},{3,2},{4,5},{5,4},{6,7},{7,6},{8,9},{9,8},{10,11... | collective-permute-start | bytes 12296 | tf_op jit(solution)/shard_map/ppermute | solution.py:686
  99.3 26.5 %collective-permute-start.18 = (bf16[512,2048]{1,0:T(8,128)(2,1)}, bf16[512,2048]{1,0:T(8,128)(2,1)}, u32[]{:S(2)}, u32[]{:S(2)}) collective-permute-start(bf16[512,2048]{1,0:T(8,128)(2,1)} %get-tuple-element.271), channel_id=1, source_target_pairs={{0,2},{1,5},{2,0},{3,7},{4,6},{5,1},{6,4},{7,3},{8,10},{9,13},{10,... | collective-permute-start | bytes 6291464 | tf_op jit(solution)/shard_map/ppermute | solution.py:686
  101.0 17.9 %collective-permute-start.19 = (bf16[256,128]{1,0:T(8,128)(2,1)S(1)}, bf16[256,128]{1,0:T(8,128)(2,1)S(1)}, u32[]{:S(2)}, u32[]{:S(2)}) collective-permute-start(bf16[256,128]{1,0:T(8,128)(2,1)S(1)} %get-tuple-element.273), channel_id=1, source_target_pairs={{0,16},{1,17},{2,18},{3,19},{4,20},{5,21},{6,22},{7,23},{8,24},{9,... | collective-permute-start | bytes 196616 | tf_op jit(solution)/shard_map/ppermute | solution.py:686
  103.7 19.2 %collective-permute-start.21 = (bf16[1024,384]{1,0:T(8,128)(2,1)}, bf16[1024,384]{1,0:T(8,128)(2,1)}, u32[]{:S(2)}, u32[]{:S(2)}) collective-permute-start(bf16[1024,384]{1,0:T(8,128)(2,1)} %get-tuple-element.277), channel_id=1, source_target_pairs={{0,8},{1,9},{2,10},{3,11},{4,12},{5,13},{6,14},{7,15},{8,0},{9,1},... | collective-permute-start | bytes 2359304 | tf_op jit(solution)/shard_map/ppermute | solution.py:686
  117.4 12.0 %collective-permute-start.17 = (bf16[1024,1024]{1,0:T(8,128)(2,1)S(1)}, bf16[1024,1024]{1,0:T(8,128)(2,1)S(1)}, u32[]{:S(2)}, u32[]{:S(2)}) collective-permute-start(bf16[1024,1024]{1,0:T(8,128)(2,1)S(1)} %get-tuple-element.269), channel_id=1, source_target_pairs={{0,1},{1,0},{2,3},{3,2},{4,5},{5,4},{6,7},{7,6},{8,9},{9,8},{10,11... | collective-permute-start | bytes 6291464 | tf_op jit(solution)/shard_map/ppermute | solution.py:686
  119.0 6.7 %collective-permute-start.20 = (bf16[128,128]{1,0:T(8,128)(2,1)S(1)}, bf16[128,128]{1,0:T(8,128)(2,1)S(1)}, u32[]{:S(2)}, u32[]{:S(2)}) collective-permute-start(bf16[128,128]{1,0:T(8,128)(2,1)S(1)} %get-tuple-element.275), channel_id=1, source_target_pairs={{0,1},{1,0},{2,3},{3,2},{4,5},{5,4},{6,7},{7,6},{8,9},{9,8},{10,11... | collective-permute-start | bytes 98312 | tf_op jit(solution)/shard_map/ppermute | solution.py:686
  124.3 5.1 %collective-permute-start.23 = (f32[8,128]{1,0:T(8,128)S(1)}, f32[8,128]{1,0:T(8,128)S(1)}, u32[]{:S(2)}, u32[]{:S(2)}) collective-permute-start(f32[8,128]{1,0:T(8,128)S(1)} %get-tuple-element.279.refs_1_), channel_id=1, source_target_pairs={{0,1},{1,0},{2,3},{3,2},{4,5},{5,4},{6,7},{7,6},{8,9},{9,8},{10,11... | collective-permute-start | bytes 12296 | tf_op jit(solution)/shard_map/ppermute | solution.py:686
  124.4 10.2 %collective-permute-start.26 = (bf16[512,384]{1,0:T(8,128)(2,1)S(1)}, bf16[512,384]{1,0:T(8,128)(2,1)S(1)}, u32[]{:S(2)}, u32[]{:S(2)}) collective-permute-start(bf16[512,384]{1,0:T(8,128)(2,1)S(1)} %get-tuple-element.287), channel_id=1, source_target_pairs={{0,4},{1,3},{2,6},{3,1},{4,0},{5,7},{6,2},{7,5},{8,12},{9,11},{10,... | collective-permute-start | bytes 1179656 | tf_op jit(solution)/shard_map/ppermute | solution.py:686
  127.8 34.9 %collective-permute-start.31 = (bf16[256,2048]{1,0:T(8,128)(2,1)S(1)}, bf16[256,2048]{1,0:T(8,128)(2,1)S(1)}, u32[]{:S(2)}, u32[]{:S(2)}) collective-permute-start(bf16[256,2048]{1,0:T(8,128)(2,1)S(1)} %get-tuple-element.297), channel_id=1, source_target_pairs={{0,8},{1,9},{2,10},{3,11},{4,12},{5,13},{6,14},{7,15},{8,0},{9,1},... | collective-permute-start | bytes 3145736 | tf_op jit(solution)/shard_map/ppermute | solution.py:686
  132.6 4.0 %collective-permute-start.25 = (bf16[1024,512]{1,0:T(8,128)(2,1)S(1)}, bf16[1024,512]{1,0:T(8,128)(2,1)S(1)}, u32[]{:S(2)}, u32[]{:S(2)}) collective-permute-start(bf16[1024,512]{1,0:T(8,128)(2,1)S(1)} %get-tuple-element.285), channel_id=1, source_target_pairs={{0,1},{1,0},{2,3},{3,2},{4,5},{5,4},{6,7},{7,6},{8,9},{9,8},{10,11... | collective-permute-start | bytes 3145736 | tf_op jit(solution)/shard_map/ppermute | solution.py:686
  134.4 6.2 %collective-permute-start.24 = (bf16[1024,512]{1,0:T(8,128)(2,1)S(1)}, bf16[1024,512]{1,0:T(8,128)(2,1)S(1)}, u32[]{:S(2)}, u32[]{:S(2)}) collective-permute-start(bf16[1024,512]{1,0:T(8,128)(2,1)S(1)} %get-tuple-element.284), channel_id=1, source_target_pairs={{0,1},{1,0},{2,3},{3,2},{4,5},{5,4},{6,7},{7,6},{8,9},{9,8},{10,11... | collective-permute-start | bytes 3145736 | tf_op jit(solution)/shard_map/ppermute | solution.py:686
  134.5 21.5 %collective-permute-start.34 = (bf16[512,1024]{1,0:T(8,128)(2,1)S(1)}, bf16[512,1024]{1,0:T(8,128)(2,1)S(1)}, u32[]{:S(2)}, u32[]{:S(2)}) collective-permute-start(bf16[512,1024]{1,0:T(8,128)(2,1)S(1)} %get-tuple-element.306), channel_id=1, source_target_pairs={{0,2},{1,5},{2,0},{3,7},{4,6},{5,1},{6,4},{7,3},{8,10},{9,13},{10,... | collective-permute-start | bytes 3145736 | tf_op jit(solution)/shard_map/ppermute | solution.py:686
  136.5 5.4 %collective-permute-start.28 = (f32[8,128]{1,0:T(8,128)S(1)}, f32[8,128]{1,0:T(8,128)S(1)}, u32[]{:S(2)}, u32[]{:S(2)}) collective-permute-start(f32[8,128]{1,0:T(8,128)S(1)} %get-tuple-element.289.refs_5_), channel_id=1, source_target_pairs={{0,1},{1,0},{2,3},{3,2},{4,5},{5,4},{6,7},{7,6},{8,9},{9,8},{10,11... | collective-permute-start | bytes 12296 | tf_op jit(solution)/shard_map/ppermute | solution.py:686
  136.6 19.3 %collective-permute-start.32 = (bf16[256,384]{1,0:T(8,128)(2,1)S(1)}, bf16[256,384]{1,0:T(8,128)(2,1)S(1)}, u32[]{:S(2)}, u32[]{:S(2)}) collective-permute-start(bf16[256,384]{1,0:T(8,128)(2,1)S(1)} %get-tuple-element.301), channel_id=1, source_target_pairs={{0,16},{1,17},{2,18},{3,19},{4,20},{5,21},{6,22},{7,23},{8,24},{9,... | collective-permute-start | bytes 589832 | tf_op jit(solution)/shard_map/ppermute | solution.py:686
  154.3 9.6 %collective-permute-start.29 = (f32[1,9216]{1,0:T(1,128)S(1)}, f32[1,9216]{1,0:T(1,128)S(1)}, u32[]{:S(2)}, u32[]{:S(2)}) collective-permute-start(f32[1,9216]{1,0:T(1,128)S(1)} %get-tuple-element.293.refs_0_), channel_id=1, source_target_pairs={{0,1},{1,0},{2,3},{3,2},{4,5},{5,4},{6,7},{7,6},{8,9},{9,8},{10,11... | collective-permute-start | bytes 110600 | tf_op jit(solution)/shard_map/ppermute | solution.py:686
  154.5 9.2 %collective-permute-start.30 = (bf16[512,512]{1,0:T(8,128)(2,1)S(1)}, bf16[512,512]{1,0:T(8,128)(2,1)S(1)}, u32[]{:S(2)}, u32[]{:S(2)}) collective-permute-start(bf16[512,512]{1,0:T(8,128)(2,1)S(1)} %get-tuple-element.295), channel_id=1, source_target_pairs={{0,2},{1,5},{2,0},{3,7},{4,6},{5,1},{6,4},{7,3},{8,10},{9,13},{10,... | collective-permute-start | bytes 1572872 | tf_op jit(solution)/shard_map/ppermute | solution.py:686
  156.1 17.7 %collective-permute-start.36 = (bf16[512,512]{1,0:T(8,128)(2,1)S(1)}, bf16[512,512]{1,0:T(8,128)(2,1)S(1)}, u32[]{:S(2)}, u32[]{:S(2)}) collective-permute-start(bf16[512,512]{1,0:T(8,128)(2,1)S(1)} %get-tuple-element.314), channel_id=1, source_target_pairs={{0,2},{1,5},{2,0},{3,7},{4,6},{5,1},{6,4},{7,3},{8,10},{9,13},{10,... | collective-permute-start | bytes 1572872 | tf_op jit(solution)/shard_map/ppermute | solution.py:686
  157.7 27.8 %collective-permute-start.41 = (bf16[256,1024]{1,0:T(8,128)(2,1)S(1)}, bf16[256,1024]{1,0:T(8,128)(2,1)S(1)}, u32[]{:S(2)}, u32[]{:S(2)}) collective-permute-start(bf16[256,1024]{1,0:T(8,128)(2,1)S(1)} %get-tuple-element.327), channel_id=1, source_target_pairs={{0,8},{1,9},{2,10},{3,11},{4,12},{5,13},{6,14},{7,15},{8,0},{9,1},... | collective-permute-start | bytes 1572872 | tf_op jit(solution)/shard_map/ppermute | solution.py:686
  162.9 12.0 %collective-permute-start.39 = (bf16[128,2048]{1,0:T(8,128)(2,1)S(1)}, bf16[128,2048]{1,0:T(8,128)(2,1)S(1)}, u32[]{:S(2)}, u32[]{:S(2)}) collective-permute-start(bf16[128,2048]{1,0:T(8,128)(2,1)S(1)} %get-tuple-element.321), channel_id=1, source_target_pairs={{0,4},{1,3},{2,6},{3,1},{4,0},{5,7},{6,2},{7,5},{8,12},{9,11},{10,... | collective-permute-start | bytes 1572872 | tf_op jit(solution)/shard_map/ppermute | solution.py:686
  163.8 11.0 %collective-permute-start.35 = (f32[1,9216]{1,0:T(1,128)S(1)}, f32[1,9216]{1,0:T(1,128)S(1)}, u32[]{:S(2)}, u32[]{:S(2)}) collective-permute-start(f32[1,9216]{1,0:T(1,128)S(1)} %get-tuple-element.312.refs_0_), channel_id=1, source_target_pairs={{0,2},{1,3},{2,0},{3,1},{4,6},{5,7},{6,4},{7,5},{8,10},{9,11},{10,... | collective-permute-start | bytes 110600 | tf_op jit(solution)/shard_map/ppermute | solution.py:686
  164.6 20.8 %collective-permute-start.38 = (bf16[256,512]{1,0:T(8,128)(2,1)S(1)}, bf16[256,512]{1,0:T(8,128)(2,1)S(1)}, u32[]{:S(2)}, u32[]{:S(2)}) collective-permute-start(bf16[256,512]{1,0:T(8,128)(2,1)S(1)} %get-tuple-element.319), channel_id=1, source_target_pairs={{0,8},{1,9},{2,10},{3,11},{4,12},{5,13},{6,14},{7,15},{8,0},{9,1},... | collective-permute-start | bytes 786440 | tf_op jit(solution)/shard_map/ppermute | solution.py:686
  173.9 19.1 %collective-permute-start.43 = (bf16[256,512]{1,0:T(8,128)(2,1)S(1)}, bf16[256,512]{1,0:T(8,128)(2,1)S(1)}, u32[]{:S(2)}, u32[]{:S(2)}) collective-permute-start(bf16[256,512]{1,0:T(8,128)(2,1)S(1)} %get-tuple-element.332), channel_id=1, source_target_pairs={{0,8},{1,9},{2,10},{3,11},{4,12},{5,13},{6,14},{7,15},{8,0},{9,1},... | collective-permute-start | bytes 786440 | tf_op jit(solution)/shard_map/ppermute | solution.py:686
  174.8 10.6 %collective-permute-start.37 = (f32[1,9216]{1,0:T(1,128)S(1)}, f32[1,9216]{1,0:T(1,128)S(1)}, u32[]{:S(2)}, u32[]{:S(2)}) collective-permute-start(f32[1,9216]{1,0:T(1,128)S(1)} %get-tuple-element.317.refs_0_), channel_id=1, source_target_pairs={{0,4},{1,5},{2,6},{3,7},{4,0},{5,1},{6,2},{7,3},{8,12},{9,13},{10,... | collective-permute-start | bytes 110600 | tf_op jit(solution)/shard_map/ppermute | solution.py:686
  175.0 23.1 %collective-permute-start.50 = (bf16[64,2048]{1,0:T(8,128)(2,1)S(1)}, bf16[64,2048]{1,0:T(8,128)(2,1)S(1)}, u32[]{:S(2)}, u32[]{:S(2)}) collective-permute-start(bf16[64,2048]{1,0:T(8,128)(2,1)S(1)} %get-tuple-element.352), channel_id=1, source_target_pairs={{0,16},{1,17},{2,18},{3,19},{4,20},{5,21},{6,22},{7,23},{8,24},{9,... | collective-permute-start | bytes 786440 | tf_op jit(solution)/shard_map/ppermute | solution.py:686
  185.4 5.1 %collective-permute-start.40 = (f32[1,9216]{1,0:T(1,128)S(1)}, f32[1,9216]{1,0:T(1,128)S(1)}, u32[]{:S(2)}, u32[]{:S(2)}) collective-permute-start(f32[1,9216]{1,0:T(1,128)S(1)} %get-tuple-element.325.refs_0_), channel_id=1, source_target_pairs={{0,8},{1,9},{2,10},{3,11},{4,12},{5,13},{6,14},{7,15},{8,0},{9,1},... | collective-permute-start | bytes 110600 | tf_op jit(solution)/shard_map/ppermute | solution.py:686
  185.7 9.8 %collective-permute-start.44 = (bf16[128,1024]{1,0:T(8,128)(2,1)S(1)}, bf16[128,1024]{1,0:T(8,128)(2,1)S(1)}, u32[]{:S(2)}, u32[]{:S(2)}) collective-permute-start(bf16[128,1024]{1,0:T(8,128)(2,1)S(1)} %get-tuple-element.337), channel_id=1, source_target_pairs={{0,4},{1,3},{2,6},{3,1},{4,0},{5,7},{6,2},{7,5},{8,12},{9,11},{10,... | collective-permute-start | bytes 786440 | tf_op jit(solution)/shard_map/ppermute | solution.py:686
  185.7 9.7 %collective-permute-start.45 = (bf16[128,512]{1,0:T(8,128)(2,1)S(1)}, bf16[128,512]{1,0:T(8,128)(2,1)S(1)}, u32[]{:S(2)}, u32[]{:S(2)}) collective-permute-start(bf16[128,512]{1,0:T(8,128)(2,1)S(1)} %get-tuple-element.339), channel_id=1, source_target_pairs={{0,4},{1,3},{2,6},{3,1},{4,0},{5,7},{6,2},{7,5},{8,12},{9,11},{10,... | collective-permute-start | bytes 393224 | tf_op jit(solution)/shard_map/ppermute | solution.py:686
  190.6 4.9 %collective-permute-start.42 = (f32[1,9216]{1,0:T(1,128)S(1)}, f32[1,9216]{1,0:T(1,128)S(1)}, u32[]{:S(2)}, u32[]{:S(2)}) collective-permute-start(f32[1,9216]{1,0:T(1,128)S(1)} %get-tuple-element.330.refs_0_), channel_id=1, source_target_pairs={{0,16},{1,17},{2,18},{3,19},{4,20},{5,21},{6,22},{7,23},{8,24},{9,... | collective-permute-start | bytes 110600 | tf_op jit(solution)/shard_map/ppermute | solution.py:686
  193.0 5.0 %collective-permute-start.47 = (bf16[128,512]{1,0:T(8,128)(2,1)S(1)}, bf16[128,512]{1,0:T(8,128)(2,1)S(1)}, u32[]{:S(2)}, u32[]{:S(2)}) collective-permute-start(bf16[128,512]{1,0:T(8,128)(2,1)S(1)} %get-tuple-element.345), channel_id=1, source_target_pairs={{0,4},{1,3},{2,6},{3,1},{4,0},{5,7},{6,2},{7,5},{8,12},{9,11},{10,... | collective-permute-start | bytes 393224 | tf_op jit(solution)/shard_map/ppermute | solution.py:686
  198.3 6.5 %collective-permute-start.49 = (bf16[64,512]{1,0:T(8,128)(2,1)S(1)}, bf16[64,512]{1,0:T(8,128)(2,1)S(1)}, u32[]{:S(2)}, u32[]{:S(2)}) collective-permute-start(bf16[64,512]{1,0:T(8,128)(2,1)S(1)} %get-tuple-element.350), channel_id=1, source_target_pairs={{0,16},{1,17},{2,18},{3,19},{4,20},{5,21},{6,22},{7,23},{8,24},{9,... | collective-permute-start | bytes 196616 | tf_op jit(solution)/shard_map/ppermute | solution.py:686
  205.5 11.4 %collective-permute-start.46 = (bf16[64,1024]{1,0:T(8,128)(2,1)S(1)}, bf16[64,1024]{1,0:T(8,128)(2,1)S(1)}, u32[]{:S(2)}, u32[]{:S(2)}) collective-permute-start(bf16[64,1024]{1,0:T(8,128)(2,1)S(1)} %get-tuple-element.343), channel_id=1, source_target_pairs={{0,16},{1,17},{2,18},{3,19},{4,20},{5,21},{6,22},{7,23},{8,24},{9,... | collective-permute-start | bytes 393224 | tf_op jit(solution)/shard_map/ppermute | solution.py:686
  205.5 11.4 %collective-permute-start.48 = (bf16[64,512]{1,0:T(8,128)(2,1)S(1)}, bf16[64,512]{1,0:T(8,128)(2,1)S(1)}, u32[]{:S(2)}, u32[]{:S(2)}) collective-permute-start(bf16[64,512]{1,0:T(8,128)(2,1)S(1)} %get-tuple-element.348), channel_id=1, source_target_pairs={{0,16},{1,17},{2,18},{3,19},{4,20},{5,21},{6,22},{7,23},{8,24},{9,... | collective-permute-start | bytes 196616 | tf_op jit(solution)/shard_map/ppermute | solution.py:686
  (30 other events, 182.0 us)
